TPU v7x, 32 devices: a whole 2x2x4 slice. The times are simulated.
32 devices in a mesh: dp: 8 (over z, x), tensor: 4 (over y, core).
Axes of the slice: x: 2, y: 2, z: 4, core: 2. Of those that a mesh axis runs over, the one named last changes fastest.
Arguments:
- inputs: bfloat16 [8, 128, 8192], P('dp'), may hold values from -6 to 6
- x_pre: bfloat16 [8, 128, 4096], P('dp', None, 'tensor'), may hold values from -6 to 6
- bc_pre: bfloat16 [8, 128, 512], P('dp', None, 'tensor'), may hold values from -6 to 6
- dt_pre: float32 [8, 128, 64], P('dp', None, 'tensor'), may hold values from -3 to 3
- gate_in: bfloat16 [8, 128, 4096], P('dp', None, 'tensor'), may hold values from -6 to 6
- conv_x: float32 [4, 4096], P(None, 'tensor'), may hold values from -3 to 3
- conv_bc: float32 [4, 512], P(None, 'tensor'), may hold values from -3 to 3
- dt_bias: float32 [64], P('tensor'), may hold values from -4 to -2
- a_log: float32 [64], P('tensor'), may hold values from -4.5 to 0
- d_skip: float32 [64], P('tensor'), may hold values from 0.5 to 1.5
- norm_w: float32 [4096], P('tensor'), may hold values from 0.5 to 1.5
- out_grad: bfloat16 [8, 128, 4096], P('dp', None, 'tensor'), may hold values from -6 to 6
- w_x: bfloat16 [8192, 4096], P('dp', 'tensor'), may hold values from -0.0625 to 0.0625
- w_bc: bfloat16 [8192, 512], P('dp', 'tensor'), may hold values from -0.0625 to 0.0625
- w_dt: bfloat16 [8192, 64], P('dp', 'tensor'), may hold values from -0.0625 to 0.0625
Outputs:
- g_inputs: bfloat16 [8, 128, 8192], P('dp', None, 'tensor')
- g_gate: bfloat16 [8, 128, 4096], P('dp', None, 'tensor')
- g_wx: bfloat16 [8192, 4096], P('dp', 'tensor')
- g_wbc: bfloat16 [8192, 512], P('dp', 'tensor')
- g_wdt: bfloat16 [8192, 64], P('dp', 'tensor')
- g_convx: float32 [4, 4096], P(None, 'tensor')
- g_convbc: float32 [4, 512], P(None, 'tensor')
- g_dtbias: float32 [64], P('tensor')
- g_alog: float32 [64], P('tensor')
- g_dskip: float32 [64], P('tensor')
- g_normw: float32 [4096], P('tensor')
All inputs are finite; a program needn't handle non-finite values.
Results may differ from a plain program's by a relative error of at most 0.015.
Values may be sent and summed in bfloat16 or wider, within the bound.
A program may use at most 128 MiB of HBM per device.

v0:
```python
import jax
import jax.numpy as jnp
from jax import lax
from jax.sharding import PartitionSpec as P

EPSILON = 1e-05
PRECISE = lax.Precision.HIGHEST


def swapped(block, axis, distance):
    count = lax.axis_size(axis)
    route = []
    for low in range(count):
        high = low | 1 << distance
        if high != low and high < count:
            route += [(low, high), (high, low)]
    return lax.ppermute(block, axis, route)


def causal_conv(values, kernel):
    kernel_width = kernel.shape[0]
    seq_len = values.shape[0]
    padded = jnp.pad(values, ((kernel_width - 1, 0), (0, 0)))
    running = jnp.zeros(values.shape, jnp.float32)
    for offset in range(kernel_width):
        running = running + kernel[offset] * padded[offset : offset + seq_len]
    return running


def state_act(pre_values, kernel):
    return jax.nn.silu(causal_conv(pre_values, kernel))


def state_mix(x_pre, b_mat, c_mat, dt_pre, gate_in, conv_x, dt_bias, a_log, d_skip):
    seq_len, channels = x_pre.shape
    head_count = dt_pre.shape[1]
    groups = b_mat.shape[1]
    per_group = head_count // groups
    head_size = channels // head_count
    mixed_x = jax.nn.silu(causal_conv(x_pre, conv_x))
    step_size = jax.nn.softplus(dt_pre + dt_bias)
    decay_rate = -jnp.exp(a_log)
    log_decay = jnp.cumsum(step_size * decay_rate, axis=0).T
    scores = jnp.einsum("tgn,sgn->gts", c_mat, b_mat, precision=PRECISE)
    scores = jnp.repeat(scores, per_group, axis=0)
    causal = jnp.arange(seq_len)[:, None] >= jnp.arange(seq_len)[None, :]
    decay_mat = jnp.exp(
        jnp.where(causal[None], log_decay[:, :, None] - log_decay[:, None, :], -jnp.inf)
    )
    weights = scores * decay_mat * step_size.T[:, None, :]
    heads_x = mixed_x.reshape(seq_len, head_count, head_size)
    result = (
        jnp.einsum("hts,shp->thp", weights, heads_x, precision=PRECISE)
        + d_skip[None, :, None] * heads_x
    )
    return result.reshape(seq_len, channels) * jax.nn.silu(gate_in)


def body(
    inputs,
    x_pre,
    bc_pre,
    dt_pre,
    gate_in,
    conv_x,
    conv_bc,
    dt_bias,
    a_log,
    d_skip,
    norm_w,
    out_grad,
    w_x,
    w_bc,
    w_dt,
):
    channels = x_pre.shape[2]
    half_width = bc_pre.shape[2]
    is_even = lax.axis_index("tensor") % 2 == 0
    bc_pre32 = bc_pre[0].astype(jnp.float32)
    own_half = state_act(bc_pre32, conv_bc).astype(jnp.bfloat16)
    far_half = swapped(own_half, "tensor", 0)
    own_float = lax.optimization_barrier(own_half).astype(jnp.float32)
    far_float = far_half.astype(jnp.float32)
    b_mat = jnp.where(is_even, own_float, far_float)[:, None, :]
    c_mat = jnp.where(is_even, far_float, own_float)[:, None, :]
    mixed_v, pullback = jax.vjp(
        state_mix,
        x_pre[0].astype(jnp.float32),
        b_mat,
        c_mat,
        dt_pre[0],
        gate_in[0].astype(jnp.float32),
        conv_x,
        dt_bias,
        a_log,
        d_skip,
    )
    upstream = out_grad[0].astype(jnp.float32)
    scaled = upstream * norm_w
    own_stats = jnp.stack([jnp.sum(mixed_v * mixed_v, axis=1), jnp.sum(scaled * mixed_v, axis=1)])
    far_stats = swapped(own_stats, "tensor", 0)
    group_stats = (own_stats + far_stats) / (2 * channels)
    inv_rms = lax.rsqrt(group_stats[0] + EPSILON)[:, None]
    grad_v = inv_rms * scaled - mixed_v * (inv_rms * inv_rms * inv_rms) * group_stats[1][:, None]
    grad_x, grad_b, grad_c, grad_dt, grad_z, grad_cx, grad_db, grad_al, grad_ds = pullback(grad_v)
    kept_grad = jnp.where(is_even, grad_b[:, 0], grad_c[:, 0])
    sent_grad = jnp.where(is_even, grad_c[:, 0], grad_b[:, 0])
    grad_own = kept_grad + swapped(sent_grad.astype(jnp.bfloat16), "tensor", 0).astype(
        sent_grad.dtype
    )
    _, pull_conv = jax.vjp(state_act, bc_pre32, conv_bc)
    grad_bcp, grad_cbc = pull_conv(grad_own)
    norm_part = jnp.sum(upstream * mixed_v * inv_rms, axis=0)
    param_grads = lax.psum((grad_cx, grad_cbc, grad_db, grad_al, grad_ds, norm_part), "dp")
    g_cat = jnp.concatenate(
        [grad_x.astype(jnp.bfloat16), grad_bcp.astype(jnp.bfloat16), grad_dt.astype(jnp.bfloat16)],
        axis=1,
    )
    w_cat = jnp.concatenate([w_x, w_bc, w_dt], axis=1)
    partial_in = lax.dot_general(
        g_cat,
        lax.all_gather(w_cat, "dp", axis=0, tiled=True),
        (((1,), (1,)), ((), ())),
        preferred_element_type=jnp.float32,
    )
    grad_in = lax.psum_scatter(
        partial_in.astype(jnp.bfloat16), "tensor", scatter_dimension=1, tiled=True
    )[None]
    full_rows = inputs[0]
    grad_w = lax.psum_scatter(
        lax.dot_general(
            full_rows, g_cat, (((0,), (0,)), ((), ())), preferred_element_type=jnp.float32
        ).astype(jnp.bfloat16),
        "dp",
        scatter_dimension=0,
        tiled=True,
    ).astype(jnp.float32)
    grad_w = grad_w.astype(jnp.bfloat16)
    return (
        grad_in,
        grad_z.astype(jnp.bfloat16)[None],
        grad_w[:, :channels],
        grad_w[:, channels : channels + half_width],
        grad_w[:, channels + half_width :],
        param_grads[0],
        param_grads[1],
        param_grads[2],
        param_grads[3],
        param_grads[4],
        param_grads[5],
    )


def solution(mesh):
    placed = (
        P("dp", None, None),
        P("dp", None, "tensor"),
        P("dp", None, "tensor"),
        P("dp", None, "tensor"),
        P("dp", None, "tensor"),
        P(None, "tensor"),
        P(None, "tensor"),
        P("tensor"),
        P("tensor"),
        P("tensor"),
        P("tensor"),
        P("dp", None, "tensor"),
        P("dp", "tensor"),
        P("dp", "tensor"),
        P("dp", "tensor"),
    )
    return jax.shard_map(
        body,
        mesh=mesh,
        in_specs=placed,
        out_specs=(
            P("dp", None, "tensor"),
            P("dp", None, "tensor"),
            P("dp", "tensor"),
            P("dp", "tensor"),
            P("dp", "tensor"),
            P(None, "tensor"),
            P(None, "tensor"),
            P("tensor"),
            P("tensor"),
            P("tensor"),
            P("tensor"),
        ),
        check_vma=False,
    )
```

profile of v0, /device:TPU:17, one launch (start us, length us, event | category | flops | bytes accessed | tf_op | source)
XLA Modules:
  0.0 776.5 jit_solution(2350530517805784917)
XLA Ops:
  8.3 3.4 pad_maximum_fusion
  16.6 1.6 reduce_window_sum.22
  18.2 1.5 copy.43
  19.7 1.5 copy.45
  23.5 4.9 multiply_reduce_fusion.7
  35.6 2.4 multiply_reduce_fusion.2
  38.0 3.0 fusion.9
  41.7 1.4 copy.52
  43.1 2.6 reduce_window_sum.23
  46.8 1.7 select_convert_fusion
  49.1 1.4 copy.51
  50.5 3.4 fusion.2
  53.9 2.0 copy.49
  55.9 1.5 fusion.66
  57.4 1.8 multiply_reduce_fusion.5
  61.1 9.3 %fusion = bf16[8192,1168]{0,1:T(8,128)(2,1)} fusion(bf16[1,128,8192]{2,1,0:T(8,128)(2,1)S(1)} %copy-done, bf16[128,16]{1,0:T(8,128)(2,1)S(1)} %get-tuple-element.54, bf16[128,128]{1,0:T(8,128)(2,1)S(1)} %fusion.54, bf16[128,1024]{1,0:T(8,128)(2,1)S(1)} %fusion.15), kind=kOutput, calls=%fused_computation.1 | convolution fusion | flops 2459938816 | bytes 21532672 | tf_op jit(solution)/shard_map/dot_general | solution.py:131
  70.5 344.6 %all-gather.2.cloned.1.call-done = bf16[8192,1168]{1,0:T(8,128)(2,1)} async-done(((bf16[1024,1168]{1,0:T(8,128)(2,1)}), bf16[8192,1168]{1,0:T(8,128)(2,1)}) %all-gather.2.cloned.1.call-update) | async-done | bytes 19136528 | tf_op jit(solution)/shard_map/all_gather | solution.py:122
  415.0 12.0 %convolution_convert_fusion.1 = bf16[128,8192]{1,0:T(8,128)(2,1)} fusion(bf16[8192,1168]{1,0:T(8,128)(2,1)} %all-gather.2.cloned.1.call-done, bf16[128,16]{1,0:T(8,128)(2,1)S(1)} %get-tuple-element.54, bf16[128,128]{1,0:T(8,128)(2,1)S(1)} %fusion.54, bf16[128,1024]{1,0:T(8,128)(2,1)S(1)} %fusion.15), kind=kOutput, calls=%fused_computation.2 | convolution fusion | flops 2451419136 | bytes 21532672 | tf_op jit(solution)/shard_map/dot_general | solution.py:120
  429.5 28.1 %all-reduce.18 = (f32[4,1024]{1,0:T(4,128)}, f32[4,128]{1,0:T(4,128)}, f32[16]{0:T(128)}, f32[16]{0:T(128)}, f32[16]{0:T(128)}, /*index=5*/f32[1024]{0:T(1024)}) all-reduce(f32[4,1024]{1,0:T(4,128)S(1)} %pad_add_fusion.6, f32[4,128]{1,0:T(4,128)S(1)} %pad_add_fusion.7, ...), channel_id=1, replica_groups=mesh['dp'=8,'tensor'=4] {'dp'}, use_global_device_ids=true, to_apply=%region_14.15 | all-reduce | flops 5680 | bytes 45440 | tf_op jit(solution)/shard_map/psum | solution.py:114
  457.6 277.7 %reduce-scatter.5.cloned.1.call-done = bf16[1024,1168]{0,1:T(8,128)(2,1)} async-done(((bf16[8192,1168]{0,1:T(8,128)(2,1)}), bf16[1024,1168]{0,1:T(8,128)(2,1)}) %reduce-scatter.5.cloned.1.call-update) | async-done | bytes 2392080 | tf_op jit(solution)/shard_map/reduce_scatter | solution.py:130
  735.3 3.2 slice.90
  738.5 4.0 copy.56
  743.3 1.4 slice.92
  744.7 25.2 %reduce-scatter.3.cloned.1.call-done = bf16[128,2048]{1,0:T(8,128)(2,1)} async-done(((bf16[128,8192]{1,0:T(8,128)(2,1)}), bf16[128,2048]{1,0:T(8,128)(2,1)}) %reduce-scatter.3.cloned.1.call-update) | async-done | bytes 524304 | tf_op jit(solution)/shard_map/reduce_scatter | solution.py:126
  (154 shorter events, 22.4 us)
Async XLA Ops:
  7.2 53.9 %copy-start = (bf16[1,128,8192]{2,1,0:T(8,128)(2,1)S(1)}, bf16[1,128,8192]{2,1,0:T(8,128)(2,1)}, u32[]{:S(2)}) copy-start(bf16[1,128,8192]{2,1,0:T(8,128)(2,1)} %param.15) | copy-start | bytes 6291460
  7.2 407.8 %all-gather.2.cloned.1.call-start = ((), (), s32[]{:S(2)}) async-start(), calls=%async_computation.2 | async-start | bytes 23592960 | tf_op jit(solution)/shard_map/all_gather | solution.py:122
  11.8 9.5 %copy-start.4 = (bf16[1,128,1024]{2,1,0:T(8,128)(2,1)S(1)}, bf16[1,128,1024]{2,1,0:T(8,128)(2,1)}, u32[]{:S(2)}) copy-start(bf16[1,128,1024]{2,1,0:T(8,128)(2,1)} %param.19) | copy-start | bytes 786436
  11.8 723.4 %reduce-scatter.5.cloned.1.call-start = ((), (), s32[]{:S(2)}) async-start(), calls=%async_computation.4 | async-start | bytes 21528576 | tf_op jit(solution)/shard_map/reduce_scatter | solution.py:130
  13.2 10.0 %collective-permute-start = (bf16[128,128]{1,0:T(8,128)(2,1)S(1)}, bf16[128,128]{1,0:T(8,128)(2,1)S(1)}, u32[]{:S(2)}, u32[]{:S(2)}) collective-permute-start(bf16[128,128]{1,0:T(8,128)(2,1)S(1)} %get-tuple-element.57), channel_id=1, source_target_pairs={{0,1},{1,0},{2,3},{3,2},{4,5},{5,4},{6,7},{7,6},{8,9},{9,8},{10,11... | collective-permute-start | bytes 98312 | tf_op jit(solution)/shard_map/ppermute | solution.py:17
  14.1 9.4 %copy-start.20 = (f32[1,1024]{1,0:T(1,128)}, f32[1,1024]{1,0:T(1,128)S(1)}, u32[]{:S(2)}) copy-start(f32[1,1024]{1,0:T(1,128)S(1)} %get-tuple-element.75) | copy-start | bytes 12292
  23.5 4.9 copy-start.17
  23.5 6.2 copy-start.3
  23.5 6.2 copy-start.19
  32.6 1.7 collective-permute-start.1
  34.3 3.7 copy-start.6
  34.3 3.8 copy-start.18
  34.3 3.8 copy-start.23
  34.3 3.8 copy-start.27
  34.3 3.8 copy-start.28
  38.0 3.1 copy-start.12
  48.5 7.4 copy-start.41
  48.5 7.4 copy-start.45
  48.5 11.2 %collective-permute-start.2 = (bf16[128,128]{1,0:T(8,128)(2,1)}, bf16[128,128]{1,0:T(8,128)(2,1)}, u32[]{:S(2)}, u32[]{:S(2)}) collective-permute-start(bf16[128,128]{1,0:T(8,128)(2,1)} %get-tuple-element.84), channel_id=1, source_target_pairs={{0,1},{1,0},{2,3},{3,2},{4,5},{5,4},{6,7},{7,6},{8,9},{9,8},{10,11... | collective-permute-start | bytes 98312 | tf_op jit(solution)/shard_map/ppermute | solution.py:17
  50.5 8.7 %copy-start.21 = (f32[1,1024]{1,0:T(1,128)S(1)}, f32[1,1024]{1,0:T(1,128)}, u32[]{:S(2)}) copy-start(f32[1,1024]{1,0:T(1,128)} %copy-done.20) | copy-start | bytes 12292
  70.4 356.7 %copy-start.2 = (f32[128,16,64]{0,2,1:T(8,128)S(1)}, f32[128,16,64]{0,2,1:T(8,128)}, u32[]{:S(2)}) copy-start(f32[128,16,64]{0,2,1:T(8,128)} %get-tuple-element.83) | copy-start | bytes 1572868
  70.4 699.5 %reduce-scatter.3.cloned.1.call-start = ((), (), s32[]{:S(2)}) async-start(), calls=%async_computation.3 | async-start | bytes 2621440 | tf_op jit(solution)/shard_map/reduce_scatter | solution.py:126
  735.3 34.7 %copy-start.1 = (bf16[1,128,8192]{2,1,0:T(8,128)(2,1)S(1)}, bf16[1,128,8192]{2,1,0:T(8,128)(2,1)}, u32[]{:S(2)}) copy-start(bf16[1,128,8192]{2,1,0:T(8,128)(2,1)} %param.15) | copy-start | bytes 6291460
  738.5 4.0 slice-start
  (35 other events, 57.4 us)
Sparse Core Ops, SparseCore 0:
  12.0 403.0 all-gather.1
  418.9 316.2 reduce-scatter.4
  738.5 31.3 reduce-scatter.2
where the time goes:
time: 779 us; the launch traced here: 776 us
  waiting for transfers between devices  648 us (83%)
  matrix products  35.7 us (5%)
  blocking collectives  28.1 us (4%)
  local copies, waits for them, and re-layouts  26.4 us (3%)
  other arithmetic  23 us (3%)
  between operations  14.4 us (2%)
    all_gather x1, waiting for transfers between devices, body(): lax.all_gather(w_cat, 'dp', axis=0, tiled=True)  345 us
    reduce_scatter x1, waiting for transfers between devices, body(): lax.psum_scatter(lax.dot_general(full_rows, g_cat, (((0,), (0,)), ((), ()...  278 us
    psum x1, blocking collectives, body(): lax.psum((grad_cx, grad_cbc, grad_db, grad_al, grad_ds, norm_part), 'dp')  28.1 us
    reduce_scatter x1, waiting for transfers between devices, body(): lax.psum_scatter(partial_in.astype(jnp.bfloat16), 'tensor', scatter_dimen...  25.2 us
  transfers between devices with their start and end apart: 6, of which 3 were waited for; matrix products, arithmetic and copies ran while one was open for 10% of the time, Pallas kernels for 0%

commit v1 on v0

--- a/solution.py
+++ b/solution.py
@@ -75,6 +75,17 @@
 ):
     channels = x_pre.shape[2]
     half_width = bc_pre.shape[2]
+    seq_len, model = inputs.shape[1:]
+    dp_size, tensor_size = lax.axis_size("dp"), lax.axis_size("tensor")
+    dp_rows = model // dp_size
+    piece = dp_rows // tensor_size
+    own_piece = lax.dynamic_index_in_dim(
+        inputs[0].reshape(seq_len, dp_size, tensor_size, piece),
+        lax.axis_index("tensor"), 2, keepdims=False,
+    ).transpose(1, 0, 2)
+    row_piece = lax.all_to_all(own_piece, "dp", 0, 0, tiled=True)
+    row_pieces = lax.all_gather(
+        row_piece.reshape(dp_size * seq_len, piece), "tensor", axis=0, tiled=False)
     is_even = lax.axis_index("tensor") % 2 == 0
     bc_pre32 = bc_pre[0].astype(jnp.float32)
     own_half = state_act(bc_pre32, conv_bc).astype(jnp.bfloat16)
@@ -111,31 +122,44 @@
     _, pull_conv = jax.vjp(state_act, bc_pre32, conv_bc)
     grad_bcp, grad_cbc = pull_conv(grad_own)
     norm_part = jnp.sum(upstream * mixed_v * inv_rms, axis=0)
-    param_grads = lax.psum((grad_cx, grad_cbc, grad_db, grad_al, grad_ds, norm_part), "dp")
+    heads = dt_pre.shape[2]
+    short = jnp.pad(
+        jnp.concatenate([grad_cbc.reshape(-1), grad_db, grad_al, grad_ds]),
+        (0, -(4 * half_width + 3 * heads) % channels)).reshape(-1, channels)
+    packed = jnp.concatenate([grad_cx, norm_part[None], short], axis=0)
+    packed = jnp.sum(lax.all_gather(packed, "dp", axis=0, tiled=False), axis=0)
+    taps = grad_cx.shape[0]
+    flat = packed[taps + 1 :].reshape(-1)
+    cut = taps * half_width
+    param_grads = (
+        packed[:taps],
+        flat[:cut].reshape(taps, half_width),
+        flat[cut : cut + heads],
+        flat[cut + heads : cut + 2 * heads],
+        flat[cut + 2 * heads : cut + 3 * heads],
+        packed[taps],
+    )
     g_cat = jnp.concatenate(
         [grad_x.astype(jnp.bfloat16), grad_bcp.astype(jnp.bfloat16), grad_dt.astype(jnp.bfloat16)],
         axis=1,
     )
+    g_all = lax.all_gather(g_cat, "dp", axis=0, tiled=True)
     w_cat = jnp.concatenate([w_x, w_bc, w_dt], axis=1)
     partial_in = lax.dot_general(
-        g_cat,
-        lax.all_gather(w_cat, "dp", axis=0, tiled=True),
-        (((1,), (1,)), ((), ())),
-        preferred_element_type=jnp.float32,
-    )
-    grad_in = lax.psum_scatter(
-        partial_in.astype(jnp.bfloat16), "tensor", scatter_dimension=1, tiled=True
-    )[None]
-    full_rows = inputs[0]
-    grad_w = lax.psum_scatter(
-        lax.dot_general(
-            full_rows, g_cat, (((0,), (0,)), ((), ())), preferred_element_type=jnp.float32
-        ).astype(jnp.bfloat16),
-        "dp",
-        scatter_dimension=0,
-        tiled=True,
-    ).astype(jnp.float32)
-    grad_w = grad_w.astype(jnp.bfloat16)
+        g_all, w_cat, (((1,), (1,)), ((), ())), preferred_element_type=jnp.float32
+    ).astype(jnp.bfloat16)
+    part = seq_len // tensor_size
+    summed = lax.psum_scatter(
+        partial_in.reshape(dp_size, tensor_size, part, dp_rows).transpose(1, 0, 2, 3)
+        .reshape(tensor_size * dp_size * part, dp_rows),
+        "tensor", scatter_dimension=0, tiled=True)
+    moved = lax.all_to_all(summed.reshape(dp_size, part, dp_rows), "dp", 0, 0, tiled=True)
+    moved = moved.transpose(1, 0, 2).reshape(part, tensor_size, model // tensor_size)
+    moved = lax.all_to_all(moved.transpose(1, 0, 2), "tensor", 0, 0, tiled=True)
+    grad_in = moved.reshape(1, seq_len, model // tensor_size)
+    grad_w = lax.dot_general(
+        row_pieces, g_all, (((1,), (0,)), ((), ())), preferred_element_type=jnp.float32
+    ).astype(jnp.bfloat16).reshape(dp_rows, -1)
     return (
         grad_in,
         grad_z.astype(jnp.bfloat16)[None],

time: 779 us -> 198 us (0.25)
  the two profiles are of different devices: /device:TPU:17 before, /device:TPU:0 now
where the time goes in v1:
time: 198 us; the launch traced here: 197 us
  waiting for transfers between devices  64 us (32%)
  blocking collectives  54.2 us (27%)
  local copies, waits for them, and re-layouts  22.3 us (11%)
  matrix products  18 us (9%)
  between operations  14.4 us (7%)
  other arithmetic  13.8 us (7%)
  starting transfers between devices  10.1 us (5%)
    all_gather x1, waiting for transfers between devices, body(): g_all = lax.all_gather(g_cat, 'dp', axis=0, tiled=True)  56.4 us
    all_gather x1, blocking collectives, body(): packed = jnp.sum(lax.all_gather(packed, 'dp', axis=0, tiled=False), axis=0)  36.7 us
    all_to_all x1, blocking collectives, body(): row_piece = lax.all_to_all(own_piece, 'dp', 0, 0, tiled=True)  17.5 us
    dot_general x3, matrix products, state_mix(): jnp.einsum('hts,shp->thp', weights, heads_x, precision=PRECISE)  7.52 us
    unnamed x84, local copies, waits for them, and re-layouts  7.37 us
    reduce_scatter x1, waiting for transfers between devices, body(): lax.psum_scatter(partial_in.reshape(dp_size, tensor_size, part, dp_rows)....  6.71 us
    all_to_all x1, starting transfers between devices, body(): lax.all_to_all(summed.reshape(dp_size, part, dp_rows), 'dp', 0, 0, tiled=...  5.53 us
    dot_general x1, matrix products, body(): lax.dot_general(g_all, w_cat, (((1,), (1,)), ((), ())), preferred_element...  5.26 us
  transfers between devices with their start and end apart: 8, of which 3 were waited for; matrix products, arithmetic and copies ran while one was open for 15% of the time, Pallas kernels for 0%

profile of v1, /device:TPU:0, one launch (start us, length us, event | category | flops | bytes accessed | tf_op | source)
XLA Modules:
  0.0 196.8 jit_solution(3287598363373315186)
XLA Ops:
  10.7 0.9 fusion.78
  11.6 1.1 copy.75
  12.7 1.4 broadcast_multiply_fusion.8
  14.1 1.2 fusion.54
  17.5 2.8 %multiply_reduce_fusion.7 = (f32[128]{0:T(128)S(1)}, f32[128,16,64]{0,2,1:T(8,128)S(1)}, f32[128,16,64]{0,2,1:T(8,128)S(1)}) fusion(bf16[128,16,64]{0,2,1:T(8,128)(2,1)S(1)} %bitcast.185, f32[128,16,64]{0,2,1:T(8,128)S(1)} %bitcast.188, f32[16]{0:T(128)} %param.24, f32[16,128]{1,0:T(8,128)} %get-tuple-element.96, f32[16,128]{1,0:T(8,128)} %copy.77, ...), kind=kOutput, calls=%fused_computation.71 | convolution fusion | flops 203685760 | bytes 1933888 | tf_op jit(solution)/shard_map/jvp(hts,shp->thp)/dot_general | solution.py:53
  23.9 1.6 multiply_reduce_fusion.2
  25.6 3.4 %fusion.20 = (f32[16,128]{1,0:T(8,128)S(1)}, f32[16,128]{1,0:T(8,128)S(1)}, f32[16,128]{1,0:T(8,128)S(1)}, f32[128,128]{1,0:T(8,128)S(1)}) fusion(f32[16,128]{1,0:T(8,128)} %get-tuple-element.96, f32[16,128]{1,0:T(8,128)} %copy.77, f32[128,128]{1,0:T(8,128)} %copy-done.4, pred[128,128]{1,0:T(8,128)(4,1)} %iota_compare_fusion, ...), kind=kOutput, calls=%fused_computation.26 | convolution fusion | flops 204711936 | bytes 1236992 | tf_op jit(solution)/shard_map/transpose(jvp(hts,shp->thp))/dot_general | solution.py:53
  29.1 1.3 fusion.13
  30.5 1.1 reduce_window_sum.23
  32.5 1.1 multiply_reduce_fusion.5
  36.5 56.4 %all-gather.5.cloned.1.call-done = bf16[1024,1168]{0,1:T(8,128)(2,1)} async-done(((bf16[128,1168]{0,1:T(8,128)(2,1)}), bf16[1024,1168]{0,1:T(8,128)(2,1)}) %all-gather.5.cloned.1.call-update) | async-done | bytes 2392080 | tf_op jit(solution)/shard_map/all_gather | solution.py:146
  92.9 5.3 %fusion.7 = bf16[1024,1024]{1,0:T(8,128)(2,1)S(1)} fusion(bf16[1024,1168]{0,1:T(8,128)(2,1)} %all-gather.5.cloned.1.call-done, bf16[1024,16]{1,0:T(8,128)(2,1)S(1)} %copy.84, bf16[1024,128]{1,0:T(8,128)(2,1)S(1)} %copy-done.35, bf16[1024,1024]{1,0:T(8,128)(2,1)} %param.27), kind=kOutput, calls=%fused_computation.8 | convolution fusion | flops 2457698304 | bytes 6881280 | tf_op jit(solution)/shard_map/dot_general | solution.py:148
  98.2 1.5 copy.85
  99.8 3.3 %reshape_squeeze.3 = bf16[128,8,4,256]{3,2,1,0:T(4,128)(2,1)S(1)} reshape(bf16[1,128,8192]{2,1,0:T(8,128)(2,1)} %param.15) | data formatting | bytes 4194304 | tf_op jit(solution)/shard_map/reshape;squeeze | solution.py:83
  103.2 1.1 constant_dynamic-slice_fusion
  104.6 17.5 %all_to_all.15 = bf16[8,128,256]{2,1,0:T(8,128)(2,1)} all-to-all(bf16[8,128,256]{2,1,0:T(8,128)(2,1)S(1)} %bitcast.186), channel_id=1, replica_groups=mesh['dp'=8,'tensor'=4] {'dp'}, dimensions={0} | all-to-all | bytes 1048576 | tf_op jit(solution)/shard_map/all_to_all | solution.py:86
  122.8 6.7 %reduce-scatter.2.cloned.1.call-done = bf16[256,1024]{1,0:T(8,128)(2,1)} async-done(((bf16[1024,1024]{1,0:T(8,128)(2,1)}), bf16[256,1024]{1,0:T(8,128)(2,1)}) %reduce-scatter.2.cloned.1.call-update) | async-done | bytes 524304 | tf_op jit(solution)/shard_map/reduce_scatter | solution.py:152
  129.5 5.5 %all-to-all-start = ((bf16[8,32,1024]{2,1,0:T(8,128)(2,1)}), bf16[8,32,1024]{2,1,0:T(8,128)(2,1)S(1)}, u32[]{:S(2)}, u32[]{:S(2)}) async-start(bf16[8,32,1024]{2,1,0:T(8,128)(2,1)} %bitcast.195), calls=%async_computation.1 | async-start | bytes 1048576 | tf_op jit(solution)/shard_map/all_to_all | solution.py:156
  135.1 0.9 copy.91
  136.1 36.7 %all-gather.1 = f32[8,6,1024]{2,1,0:T(8,128)S(1)} all-gather(f32[1,6,1024]{2,1,0:T(8,128)S(1)} %maximum_bitcast_fusion), channel_id=2, replica_groups=mesh['dp'=8,'tensor'=4] {'dp'}, dimensions={0}, use_global_device_ids=true | all-gather | bytes 221184 | tf_op jit(solution)/shard_map/all_gather | solution.py:130
  175.9 1.1 copy.87
  177.0 3.5 %all-to-all-start.1 = ((bf16[4,32,2048]{2,1,0:T(8,128)(2,1)}), bf16[4,32,2048]{2,1,0:T(8,128)(2,1)S(1)}, u32[]{:S(2)}, u32[]{:S(2)}) async-start(bf16[4,32,2048]{2,1,0:T(8,128)(2,1)} %copy.87), calls=%async_computation.2 | async-start | bytes 1048576 | tf_op jit(solution)/shard_map/all_to_all | solution.py:158
  180.5 4.4 %fusion.10 = bf16[4,146,8,256]{3,2,1,0:T(8,128)(2,1)S(1)} fusion(bf16[4,1024,256]{2,1,0:T(8,128)(2,1)} %all-gather.7.cloned.1.call-done, bf16[1024,1168]{0,1:T(8,128)(2,1)S(1)} %copy-done.34), kind=kOutput, calls=%fused_computation.9 | convolution fusion | flops 2450669568 | bytes 6881280 | tf_op jit(solution)/shard_map/dot_general | solution.py:160
  186.1 2.6 %copy.92 = bf16[1024,1024]{1,0:T(8,128)(2,1)} copy(bf16[1024,1024]{0,1:T(8,128)(2,1)S(1)} %slice.132) | data formatting | bytes 4194304
  (144 shorter events, 20.0 us)
Async XLA Ops:
  7.2 9.7 %copy-start = (bf16[1,128,1024]{2,1,0:T(8,128)(2,1)S(1)}, bf16[1,128,1024]{2,1,0:T(8,128)(2,1)}, u32[]{:S(2)}) copy-start(bf16[1,128,1024]{2,1,0:T(8,128)(2,1)} %param.19) | copy-start | bytes 786436
  7.2 9.9 %copy-start.1 = (bf16[1,128,1024]{2,1,0:T(8,128)(2,1)S(1)}, bf16[1,128,1024]{2,1,0:T(8,128)(2,1)}, u32[]{:S(2)}) copy-start(bf16[1,128,1024]{2,1,0:T(8,128)(2,1)} %param.26) | copy-start | bytes 786436
  7.2 85.7 %all-gather.5.cloned.1.call-start = ((), (), s32[]{:S(2)}) async-start(), calls=%async_computation.4 | async-start | bytes 2691072 | tf_op jit(solution)/shard_map/all_gather | solution.py:146
  8.1 9.4 %copy-start.23 = (f32[128]{0:T(128)}, f32[128]{0:T(128)S(1)}, u32[]{:S(2)}) copy-start(f32[128]{0:T(128)S(1)} %get-tuple-element.100) | copy-start | bytes 1540
  9.5 7.7 %collective-permute-start = (bf16[128,128]{1,0:T(8,128)(2,1)S(1)}, bf16[128,128]{1,0:T(8,128)(2,1)S(1)}, u32[]{:S(2)}, u32[]{:S(2)}) collective-permute-start(bf16[128,128]{1,0:T(8,128)(2,1)S(1)} %get-tuple-element.75), channel_id=1, source_target_pairs={{0,1},{1,0},{2,3},{3,2},{4,5},{5,4},{6,7},{7,6},{8,9},{9,8},{10,11... | collective-permute-start | bytes 98312 | tf_op jit(solution)/shard_map/ppermute | solution.py:17
  10.7 5.3 %copy-start.28 = (f32[16]{0:T(128)}, f32[16]{0:T(128)S(1)}, u32[]{:S(2)}) copy-start(f32[16]{0:T(128)S(1)} %exponential_negate_fusion) | copy-start | bytes 196
  11.6 4.4 %copy-start.7 = (f32[1,1024]{1,0:T(1,128)}, f32[1,1024]{1,0:T(1,128)S(1)}, u32[]{:S(2)}) copy-start(f32[1,1024]{1,0:T(1,128)S(1)} %get-tuple-element.94) | copy-start | bytes 12292
  21.7 1.5 collective-permute-start.1
  25.6 3.5 %copy-start.5 = (f32[128,128]{1,0:T(8,128)S(1)}, f32[128,128]{1,0:T(8,128)}, u32[]{:S(2)}) copy-start(f32[128,128]{1,0:T(8,128)} %copy-done.4) | copy-start | bytes 196612
  25.6 3.5 %copy-start.11 = (pred[128,128]{1,0:T(8,128)(4,1)S(1)}, pred[128,128]{1,0:T(8,128)(4,1)}, u32[]{:S(2)}) copy-start(pred[128,128]{1,0:T(8,128)(4,1)} %iota_compare_fusion) | copy-start | bytes 49156
  25.6 3.5 %copy-start.12 = (f32[16,128]{1,0:T(8,128)S(1)}, f32[16,128]{1,0:T(8,128)}, u32[]{:S(2)}) copy-start(f32[16,128]{1,0:T(8,128)} %get-tuple-element.96) | copy-start | bytes 24580
  29.1 4.5 %copy-start.8 = (f32[1,1024]{1,0:T(1,128)S(1)}, f32[1,1024]{1,0:T(1,128)}, u32[]{:S(2)}) copy-start(f32[1,1024]{1,0:T(1,128)} %copy-done.7) | copy-start | bytes 12292
  32.2 2.8 %collective-permute-start.2 = (bf16[128,128]{1,0:T(8,128)(2,1)S(1)}, bf16[128,128]{1,0:T(8,128)(2,1)S(1)}, u32[]{:S(2)}, u32[]{:S(2)}) collective-permute-start(bf16[128,128]{1,0:T(8,128)(2,1)S(1)} %get-tuple-element.104), channel_id=1, source_target_pairs={{0,1},{1,0},{2,3},{3,2},{4,5},{5,4},{6,7},{7,6},{8,9},{9,8},{10,11... | collective-permute-start | bytes 98312 | tf_op jit(solution)/shard_map/ppermute | solution.py:17
  34.2 58.7 %copy-start.35 = (bf16[1024,128]{1,0:T(8,128)(2,1)S(1)}, bf16[1024,128]{1,0:T(8,128)(2,1)}, u32[]{:S(2)}) copy-start(bf16[1024,128]{1,0:T(8,128)(2,1)} %param.28) | copy-start | bytes 786436
  36.1 93.4 %reduce-scatter.2.cloned.1.call-start = ((), (), s32[]{:S(2)}) async-start(), calls=%async_computation.5 | async-start | bytes 2621440 | tf_op jit(solution)/shard_map/reduce_scatter | solution.py:152
  99.8 80.7 %all-gather.7.cloned.1.call-start = ((), (), s32[]{:S(2)}) async-start(), calls=%async_computation.6 | async-start | bytes 2621440 | tf_op jit(solution)/shard_map/all_gather | solution.py:87
  103.1 19.0 %copy-start.15 = (f32[128]{0:T(128)S(1)}, f32[128]{0:T(128)}, u32[]{:S(2)}) copy-start(f32[128]{0:T(128)} %copy-done.14) | copy-start | bytes 1540
  104.3 18.1 %copy-start.26 = (f32[128]{0:T(128)S(1)}, f32[128]{0:T(128)}, u32[]{:S(2)}) copy-start(f32[128]{0:T(128)} %copy-done.25) | copy-start | bytes 1540
  104.3 18.1 %copy-start.32 = (f32[128]{0:T(128)S(1)}, f32[128]{0:T(128)}, u32[]{:S(2)}) copy-start(f32[128]{0:T(128)} %copy-done.31) | copy-start | bytes 1540
  122.1 13.9 %copy-start.37 = (f32[16]{0:T(128)S(1)}, f32[16]{0:T(128)}, u32[]{:S(2)}) copy-start(f32[16]{0:T(128)} %param.23) | copy-start | bytes 196
  122.1 13.9 %copy-start.33 = (f32[16]{0:T(128)S(1)}, f32[16]{0:T(128)}, u32[]{:S(2)}) copy-start(f32[16]{0:T(128)} %get-tuple-element.71) | copy-start | bytes 196
  129.5 45.7 %all-to-all-start = ((bf16[8,32,1024]{2,1,0:T(8,128)(2,1)}), bf16[8,32,1024]{2,1,0:T(8,128)(2,1)S(1)}, u32[]{:S(2)}, u32[]{:S(2)}) async-start(bf16[8,32,1024]{2,1,0:T(8,128)(2,1)} %bitcast.195), calls=%async_computation.1 | async-start | bytes 1048576 | tf_op jit(solution)/shard_map/all_to_all | solution.py:156
  136.1 44.4 %copy-start.34 = (bf16[1024,1168]{0,1:T(8,128)(2,1)S(1)}, bf16[1024,1168]{0,1:T(8,128)(2,1)}, u32[]{:S(2)}) copy-start(bf16[1024,1168]{0,1:T(8,128)(2,1)} %all-gather.5.cloned.1.call-done) | copy-start | bytes 7176196
  177.0 12.5 %all-to-all-start.1 = ((bf16[4,32,2048]{2,1,0:T(8,128)(2,1)}), bf16[4,32,2048]{2,1,0:T(8,128)(2,1)S(1)}, u32[]{:S(2)}, u32[]{:S(2)}) async-start(bf16[4,32,2048]{2,1,0:T(8,128)(2,1)} %copy.87), calls=%async_computation.2 | async-start | bytes 1048576 | tf_op jit(solution)/shard_map/all_to_all | solution.py:158
  (22 other events, 42.2 us)
Sparse Core Ops, SparseCore 0:
  36.2 56.6 all-gather.4
  99.9 29.5 reduce-scatter.1
  131.2 22.5 all-gather.6

commit v2 on v1

--- a/solution.py
+++ b/solution.py
@@ -1,7 +1,10 @@
 import jax
 import jax.numpy as jnp
 from jax import lax
+from jax.experimental import pallas as pl
+from jax.experimental.pallas import tpu as pltpu
 from jax.sharding import PartitionSpec as P
+import functools
 
 EPSILON = 1e-05
 PRECISE = lax.Precision.HIGHEST
@@ -54,6 +57,226 @@
         + d_skip[None, :, None] * heads_x
     )
     return result.reshape(seq_len, channels) * jax.nn.silu(gate_in)
+
+
+def ring_index(place, count):
+    place = lax.rem(place + 2 * count, count)
+    return jnp.where(place < count // 2, 2 * place, 2 * (count - 1 - place) + 1)
+
+
+def exchange_kernel(
+    n, m, g_ref, w_ref, q_ref, all_ref, sum_ref, out_ref,
+    part_buf, far_buf, red_buf, q_buf,
+    ring_send, ring_recv, q_send, q_recv, far_send, far_recv, red_send, red_recv,
+):
+    d, t = lax.axis_index("dp"), lax.axis_index("tensor")
+    seq_len = g_ref.shape[0]
+    part = seq_len // m
+    ratio = n // m
+    goal = d // ratio
+    column = lax.rem(d, ratio)
+    place = jnp.where(lax.rem(d, 2) == 0, d // 2, n - 1 - d // 2)
+    right, left = ring_index(place + 1, n), ring_index(place - 1, n)
+    right_steps = n // 2
+    left_steps = n - 1 - right_steps
+    barrier = pltpu.get_barrier_semaphore()
+
+    def signal(dp, tensor):
+        pl.semaphore_signal(
+            barrier, inc=1, device_id={"dp": dp, "tensor": tensor},
+            device_id_type=pl.DeviceIdType.MESH)
+
+    def greet_dp(k, c):
+        signal(lax.rem(d + k, n), t)
+        return c
+
+    def greet_tensor(k, c):
+        signal(d, lax.rem(t + k, m))
+        return c
+
+    def greet_out(s, c):
+        @pl.when(jnp.logical_or(s != d, goal != t))
+        def _():
+            signal(s, goal)
+        return c
+
+    def greet_in(i, c):
+        source, other = t * ratio + i // m, lax.rem(i, m)
+
+        @pl.when(jnp.logical_or(source != d, other != t))
+        def _():
+            signal(source, other)
+        return c
+
+    lax.fori_loop(1, n, greet_dp, 0)
+    lax.fori_loop(1, m, greet_tensor, 0)
+    lax.fori_loop(0, n, greet_out, 0)
+    lax.fori_loop(0, ratio * m, greet_in, 0)
+    all_ref[0] = g_ref[...]
+    q_buf[0] = q_ref[...]
+    is_self = (goal == t).astype(jnp.int32)
+    pl.semaphore_wait(barrier, (n - 1) + (m - 1) + n + ratio * m - 2 * is_self)
+
+    def q_copy(k):
+        return pltpu.make_async_remote_copy(
+            src_ref=q_ref, dst_ref=q_buf.at[k], send_sem=q_send.at[k], recv_sem=q_recv.at[k],
+            device_id={"dp": lax.rem(d + k, n)}, device_id_type=pl.DeviceIdType.MESH)
+
+    def ring_copy(way, k):
+        source = ring_index(place - k if way == 0 else place + k, n)
+        target = right if way == 0 else left
+        return pltpu.make_async_remote_copy(
+            src_ref=all_ref.at[lax.rem(d - source + n, n)],
+            dst_ref=all_ref.at[lax.rem(target - source + n, n)],
+            send_sem=ring_send.at[way, k], recv_sem=ring_recv.at[way, k],
+            device_id={"dp": target}, device_id_type=pl.DeviceIdType.MESH)
+
+    def far_copy(j, k):
+        other = lax.rem(t + k, m)
+        return pltpu.make_async_remote_copy(
+            src_ref=part_buf.at[j, other], dst_ref=far_buf.at[j, k],
+            send_sem=far_send.at[j, k], recv_sem=far_recv.at[j, k],
+            device_id={"tensor": other}, device_id_type=pl.DeviceIdType.MESH)
+
+    def out_copy(j, s):
+        return pltpu.make_async_remote_copy(
+            src_ref=red_buf.at[j], dst_ref=out_ref.at[column, t],
+            send_sem=red_send.at[j], recv_sem=red_recv.at[column, t],
+            device_id={"dp": s, "tensor": goal}, device_id_type=pl.DeviceIdType.MESH)
+
+    def source_of(j):
+        k = (j + 1) // 2
+        return ring_index(jnp.where(lax.rem(j, 2) == 1, place - k, place + k), n)
+
+    def is_remote(s):
+        return jnp.logical_or(s != d, goal != t)
+
+    ring_copy(0, 0).start()
+    ring_copy(1, 0).start()
+
+    def q_start(k, c):
+        q_copy(k).start()
+        return c
+
+    lax.fori_loop(1, n, q_start, 0)
+
+    def reduce(j):
+        total = part_buf[j, t].astype(jnp.float32)
+        for k in range(1, m):
+            far_copy(j, k).wait_recv()
+            total = total + far_buf[j, k].astype(jnp.float32)
+        red_buf[j] = total.astype(jnp.bfloat16)
+        s = source_of(j)
+
+        @pl.when(is_remote(s))
+        def _():
+            out_copy(j, s).start()
+
+        @pl.when(jnp.logical_not(is_remote(s)))
+        def _():
+            out_ref[column, t] = red_buf[j]
+
+    def step(j, c):
+        k = j // 2
+
+        @pl.when(lax.rem(j, 2) == 1)
+        def _():
+            ring_copy(0, k).wait_recv()
+
+            @pl.when(k + 1 < right_steps)
+            def _():
+                ring_copy(0, k + 1).start()
+
+        @pl.when(jnp.logical_and(lax.rem(j, 2) == 0, j > 0))
+        def _():
+            ring_copy(1, k - 1).wait_recv()
+
+            @pl.when(k < left_steps)
+            def _():
+                ring_copy(1, k).start()
+
+        slot = lax.rem(d - source_of(j) + n, n)
+        product = lax.dot_general(
+            all_ref[slot], w_ref[...], (((1,), (1,)), ((), ())),
+            preferred_element_type=jnp.float32)
+        part_buf[j] = product.reshape(m, part, product.shape[1]).astype(jnp.bfloat16)
+        for hop in range(1, m):
+            far_copy(j, hop).start()
+
+        @pl.when(j > 0)
+        def _():
+            reduce(j - 1)
+        return c
+
+    lax.fori_loop(0, n, step, 0)
+    reduce(n - 1)
+
+    def q_finish(k, c):
+        q_copy(k).wait()
+        return c
+
+    lax.fori_loop(1, n, q_finish, 0)
+    sum_ref[...] = jnp.sum(q_buf[...], axis=0)
+    for k in range(right_steps):
+        ring_copy(0, k).wait_send()
+    for k in range(left_steps):
+        ring_copy(1, k).wait_send()
+
+    def drain(j, c):
+        for k in range(1, m):
+            far_copy(j, k).wait_send()
+        s = source_of(j)
+
+        @pl.when(is_remote(s))
+        def _():
+            out_copy(j, s).wait_send()
+        return c
+
+    lax.fori_loop(0, n, drain, 0)
+
+    def arrive(i, c):
+        r, other = i // m, lax.rem(i, m)
+
+        @pl.when(jnp.logical_or(t * ratio + r != d, other != t))
+        def _():
+            pltpu.make_async_remote_copy(
+                src_ref=red_buf.at[0], dst_ref=out_ref.at[r, other],
+                send_sem=red_send.at[0], recv_sem=red_recv.at[r, other],
+                device_id={"dp": t * ratio + r, "tensor": other},
+                device_id_type=pl.DeviceIdType.MESH).wait_recv()
+        return c
+
+    lax.fori_loop(0, ratio * m, arrive, 0)
+
+
+def exchange(g_cat, w_cat, packed, n, m):
+    seq_len, width = g_cat.shape
+    rows = w_cat.shape[0]
+    part = seq_len // m
+    vmem = pl.BlockSpec(memory_space=pltpu.VMEM)
+    dma = pltpu.SemaphoreType.DMA
+    return pl.pallas_call(
+        functools.partial(exchange_kernel, n, m),
+        out_shape=(
+            jax.ShapeDtypeStruct((n, seq_len, width), jnp.bfloat16),
+            jax.ShapeDtypeStruct(packed.shape, jnp.float32),
+            jax.ShapeDtypeStruct((n // m, m, part, rows), jnp.bfloat16),
+        ),
+        in_specs=[vmem] * 3,
+        out_specs=[vmem] * 3,
+        scratch_shapes=[
+            pltpu.VMEM((n, m, part, rows), jnp.bfloat16),
+            pltpu.VMEM((n, m, part, rows), jnp.bfloat16),
+            pltpu.VMEM((n, part, rows), jnp.bfloat16),
+            pltpu.VMEM((n,) + packed.shape, jnp.float32),
+            dma((2, n)), dma((2, n)), dma((n,)), dma((n,)),
+            dma((n, m)), dma((n, m)), dma((n,)), dma((n // m, m)),
+        ],
+        compiler_params=pltpu.CompilerParams(
+            collective_id=0, has_side_effects=True, vmem_limit_bytes=40 * 2**20),
+        cost_estimate=pl.CostEstimate(
+            flops=2 * n * seq_len * width * rows, bytes_accessed=60 * 2**20, transcendentals=0),
+    )(g_cat, w_cat, packed)
 
 
 def body(
@@ -78,14 +301,15 @@
     seq_len, model = inputs.shape[1:]
     dp_size, tensor_size = lax.axis_size("dp"), lax.axis_size("tensor")
     dp_rows = model // dp_size
-    piece = dp_rows // tensor_size
-    own_piece = lax.dynamic_index_in_dim(
-        inputs[0].reshape(seq_len, dp_size, tensor_size, piece),
-        lax.axis_index("tensor"), 2, keepdims=False,
-    ).transpose(1, 0, 2)
-    row_piece = lax.all_to_all(own_piece, "dp", 0, 0, tiled=True)
-    row_pieces = lax.all_gather(
-        row_piece.reshape(dp_size * seq_len, piece), "tensor", axis=0, tiled=False)
+    here = lax.axis_index("dp")
+
+    def rows_of(owner):
+        return lax.dynamic_slice_in_dim(inputs[0], owner * dp_rows, dp_rows, axis=1)
+
+    rows = [rows_of(here)]
+    for hop in range(1, dp_size):
+        route = [(i, (i + hop) % dp_size) for i in range(dp_size)]
+        rows.append(lax.ppermute(rows_of(lax.rem(here + hop, dp_size)), "dp", route))
     is_even = lax.axis_index("tensor") % 2 == 0
     bc_pre32 = bc_pre[0].astype(jnp.float32)
     own_half = state_act(bc_pre32, conv_bc).astype(jnp.bfloat16)
@@ -127,7 +351,16 @@
         jnp.concatenate([grad_cbc.reshape(-1), grad_db, grad_al, grad_ds]),
         (0, -(4 * half_width + 3 * heads) % channels)).reshape(-1, channels)
     packed = jnp.concatenate([grad_cx, norm_part[None], short], axis=0)
-    packed = jnp.sum(lax.all_gather(packed, "dp", axis=0, tiled=False), axis=0)
+    packed = jnp.pad(packed, ((0, -packed.shape[0] % 8), (0, 0)))
+    width = channels + half_width + heads
+    pad = -width % 128
+    g_cat = jnp.concatenate(
+        [grad_x.astype(jnp.bfloat16), grad_bcp.astype(jnp.bfloat16), grad_dt.astype(jnp.bfloat16),
+         jnp.zeros((seq_len, pad), jnp.bfloat16)],
+        axis=1,
+    )
+    w_cat = jnp.concatenate([w_x, w_bc, w_dt, jnp.zeros((dp_rows, pad), jnp.bfloat16)], axis=1)
+    g_all, packed, moved = exchange(g_cat, w_cat, packed, dp_size, tensor_size)
     taps = grad_cx.shape[0]
     flat = packed[taps + 1 :].reshape(-1)
     cut = taps * half_width
@@ -139,27 +372,13 @@
         flat[cut + 2 * heads : cut + 3 * heads],
         packed[taps],
     )
-    g_cat = jnp.concatenate(
-        [grad_x.astype(jnp.bfloat16), grad_bcp.astype(jnp.bfloat16), grad_dt.astype(jnp.bfloat16)],
-        axis=1,
-    )
-    g_all = lax.all_gather(g_cat, "dp", axis=0, tiled=True)
-    w_cat = jnp.concatenate([w_x, w_bc, w_dt], axis=1)
-    partial_in = lax.dot_general(
-        g_all, w_cat, (((1,), (1,)), ((), ())), preferred_element_type=jnp.float32
-    ).astype(jnp.bfloat16)
-    part = seq_len // tensor_size
-    summed = lax.psum_scatter(
-        partial_in.reshape(dp_size, tensor_size, part, dp_rows).transpose(1, 0, 2, 3)
-        .reshape(tensor_size * dp_size * part, dp_rows),
-        "tensor", scatter_dimension=0, tiled=True)
-    moved = lax.all_to_all(summed.reshape(dp_size, part, dp_rows), "dp", 0, 0, tiled=True)
-    moved = moved.transpose(1, 0, 2).reshape(part, tensor_size, model // tensor_size)
-    moved = lax.all_to_all(moved.transpose(1, 0, 2), "tensor", 0, 0, tiled=True)
-    grad_in = moved.reshape(1, seq_len, model // tensor_size)
+    grad_in = moved.transpose(1, 2, 0, 3).reshape(1, seq_len, model // tensor_size)
     grad_w = lax.dot_general(
-        row_pieces, g_all, (((1,), (0,)), ((), ())), preferred_element_type=jnp.float32
-    ).astype(jnp.bfloat16).reshape(dp_rows, -1)
+        jnp.concatenate(rows, axis=0),
+        g_all.reshape(dp_size * seq_len, width + pad),
+        (((0,), (0,)), ((), ())),
+        preferred_element_type=jnp.float32,
+    ).astype(jnp.bfloat16)[:, :width]
     return (
         grad_in,
         grad_z.astype(jnp.bfloat16)[None],

time: 198 us -> 153 us (0.77)
  the two profiles are of different devices: /device:TPU:0 before, /device:TPU:27 now
where the time goes in v2:
time: 153 us; the launch traced here: 152 us
  Pallas kernels  51.6 us (34%)
  local copies, waits for them, and re-layouts  39.6 us (26%)
  other arithmetic  19.6 us (13%)
  matrix products  14.8 us (10%)
  starting transfers between devices  13.1 us (9%)
  waiting for transfers between devices  12.2 us (8%)
    pallas_call x1, Pallas kernels, exchange(): pl.pallas_call(functools.partial(exchange_kernel, n, m), out_shape=(jax.S...  51.6 us
    unnamed x118, local copies, waits for them, and re-layouts  13.4 us
    ppermute x7, waiting for transfers between devices, body(): lax.ppermute(rows_of(lax.rem(here + hop, dp_size)), 'dp', route)  12.2 us
    ppermute x7, starting transfers between devices, body(): lax.ppermute(rows_of(lax.rem(here + hop, dp_size)), 'dp', route)  11.5 us
    dot_general x3, matrix products, state_mix(): jnp.einsum('hts,shp->thp', weights, heads_x, precision=PRECISE)  7.14 us
    dot_general x1, matrix products, body(): lax.dot_general(jnp.concatenate(rows, axis=0), g_all.reshape(dp_size * se...  4.57 us
    concatenate x1, local copies, waits for them, and re-layouts, body(): jnp.concatenate([w_x, w_bc, w_dt, jnp.zeros((dp_rows, pad), jnp.bfloat16)...  3.74 us
    dot_general x3, matrix products, state_mix(): scores = jnp.einsum('tgn,sgn->gts', c_mat, b_mat, precision=PRECISE)  3.1 us
  transfers between devices with their start and end apart: 10, of which 1 were waited for; matrix products, arithmetic and copies ran while one was open for 40% of the time, Pallas kernels for 34%

profile of v2, /device:TPU:27, one launch (start us, length us, event | category | flops | bytes accessed | tf_op | source)
XLA Modules:
  0.0 152.2 jit_solution(7958998977447142373)
XLA Ops:
  3.7 2.7 %dynamic-slice_bitcast_fusion = (bf16[128,1024]{1,0:T(8,128)(2,1)}, bf16[128,1024]{1,0:T(8,128)(2,1)}, bf16[128,1024]{1,0:T(8,128)(2,1)}, bf16[128,1024]{1,0:T(8...) fusion(bf16[1,128,8192]{2,1,0:T(8,128)(2,1)} %param.15, ...), kind=kLoop, calls=%fused_computation.78 | loop fusion | bytes 3670044 | tf_op jit(solution)/shard_map/dynamic_slice | solution.py:307
  7.7 2.3 %collective-permute-start.5 = (bf16[128,1024]{1,0:T(8,128)(2,1)}, bf16[128,1024]{1,0:T(8,128)(2,1)}, u32[]{:S(2)}, u32[]{:S(2)}) collective-permute-start(bf16[128,1024]{1,0:T(8,128)(2,1)} %get-tuple-element.75), channel_id=1, source_target_pairs={{0,12},{4,16},{8,20},{12,24},{16,28},{20,0},{24,4},{28,8},{1,13},{... | collective-permute-start | bytes 786440 | tf_op jit(solution)/shard_map/ppermute | solution.py:312
  13.5 2.0 %multiply_reduce_fusion.7 = (f32[128]{0:T(128)S(1)}, f32[128,16,64]{0,2,1:T(8,128)S(1)}) fusion(f32[128,16,64]{0,2,1:T(8,128)S(1)} %bitcast.148, f32[128,16,64]{0,2,1:T(8,128)S(1)} %bitcast.145, f32[16]{0:T(128)S(1)} %copy-done.51, f32[16,128]{1,0:T(8,128)S(1)} %copy.61, f32[16,128]{1,0:T(8,128)S(1)} %copy.59, f32[128,128]{1,0:T(8,128)S(1)} %fusion.54, ...), kind=kOutput, calls=%fused_computation.56 | convolution fusion | flops 203554688 | bytes 1671744 | tf_op jit(solution)/shard_map/jvp(hts,shp->thp)/dot_general | solution.py:56
  17.5 1.7 %bitcast_dynamic-update-slice_fusion = bf16[1024,1024]{1,0:T(8,128)(2,1)} fusion(bf16[1,128,8192]{2,1,0:T(8,128)(2,1)} %param.15, s32[]{:T(128)S(6)} %select_n.82), kind=kLoop, calls=%fused_computation.76 | loop fusion | bytes 524292
  22.4 3.7 %concatenate.16.w_ref = bf16[1024,1280]{1,0:T(8,128)(2,1)S(1)} concatenate(bf16[1024,1024]{1,0:T(8,128)(2,1)} %param.27, bf16[1024,128]{1,0:T(8,128)(2,1)} %param.28, bf16[1024,16]{1,0:T(8,128)(2,1)} %copy.69, bf16[1024,112]{1,0:T(8,128)(2,1)} %broadcast_in_dim.28), dimensions={1} | concatenate | bytes 5242880 | tf_op jit(solution)/shard_map/concatenate | solution.py:362
  26.1 2.1 %copy.72 = f32[1,128,1024]{2,1,0:T(8,128)} copy(f32[1,128,1024]{1,2,0:T(8,128)} %bitcast.144) | data formatting | bytes 1048576 | tf_op jit(solution)/shard_map/jvp()/reshape | solution.py:59
  29.0 1.9 %fusion.32 = f32[1024]{0:T(1024)} fusion(bf16[1,128,1024]{2,1,0:T(8,128)(2,1)S(1)} %copy-done.4, f32[128]{0:T(128)S(1)} %get-tuple-element.101, f32[128,1024]{1,0:T(8,128)} %copy-done.3, bf16[1,128,1024]{2,1,0:T(8,128)(2,1)} %param.19), kind=kLoop, calls=%fused_computation.49 | loop fusion | flops 1309696 | bytes 1053184 | tf_op jit(solution)/shard_map/reduce_sum | solution.py:348
  30.9 2.4 %multiply_reduce_fusion.2 = (f32[16]{0:T(128)}, f32[128,16,64]{0,2,1:T(8,128)S(1)}) fusion(f32[128,16,64]{0,2,1:T(8,128)} %bitcast.146, f32[128]{0:T(128)S(1)} %get-tuple-element.102, f32[128]{0:T(128)S(1)} %multiply_multiply_fusion, f32[128,16,64]{0,2,1:T(8,128)} %copy-done.2, f32[128,16,64]{0,2,1:T(8,128)} %bitcast.149, f32[128,16,64]{0,2,1:T(8,128)} %bitcast.150, ...), kind=kLoop, calls=%fused_computation.50 | loop fusion | flops 1703920 | bytes 2627136 | tf_op jit(solution)/shard_map/transpose(jvp())/reduce_sum | solution.py:57
  33.4 3.0 %fusion.7 = (f32[16,128]{1,0:T(8,128)S(1)}, f32[16,128]{1,0:T(8,128)S(1)}, f32[16,128]{1,0:T(8,128)}, f32[128,128]{1,0:T(8,128)}) fusion(f32[16,128]{1,0:T(8,128)S(1)} %copy-done.35, f32[16,128]{1,0:T(8,128)S(1)} %copy-done.33, f32[128,128]{1,0:T(8,128)S(1)} %copy-done.21, pred[128,128]{1,0:T(8,128)(4,1)S(1)} %copy-done.29, ...), kind=kOutput, calls=%fused_computation.14 | convolution fusion | flops 204711936 | bytes 1236992 | tf_op jit(solution)/shard_map/transpose(jvp(hts,shp->thp))/dot_general | solution.py:56
  36.4 2.1 %fusion = f32[128,16,64]{0,2,1:T(8,128)} fusion(f32[128,16,64]{0,2,1:T(8,128)S(1)} %get-tuple-element.67, f32[16,128]{1,0:T(8,128)S(1)} %copy-done.35, f32[16,128]{1,0:T(8,128)S(1)} %copy-done.33, f32[128,128]{1,0:T(8,128)S(1)} %copy-done.21, pred[128,128]{1,0:T(8,128)(4,1)S(1)} %copy-done.29, f32[16]{0:T(128)S(1)} %copy-done.52), kind=kOutput, calls=%fused_computation.2 | convolution fusion | flops 202637312 | bytes 1146944 | tf_op jit(solution)/shard_map/transpose(jvp(hts,shp->thp))/dot_general | solution.py:56
  40.5 2.6 %reduce_window_sum.23 = f32[128,16]{1,0:T(8,128)} reduce-window(f32[128,16]{1,0:T(8,128)} %copy.68, f32[]{:T(128)} %constant.79.clone.1), window={size=128x1 pad=0_127x0_0}, to_apply=%region_7.8 | reduce-window | flops 260096 | bytes 16388 | tf_op jit(solution)/shard_map/transpose(jvp(jit(cumsum)))/reduce_window_sum | solution.py:46
  44.2 1.7 %select_convert_fusion = (bf16[128,128]{1,0:T(8,128)(2,1)}, f32[128,128]{1,0:T(8,128)}) fusion(f32[128,128]{1,0:T(8,128)S(1)} %fusion.53, pred[]{:T(512)S(6)} %eq.13, f32[128,128]{1,0:T(8,128)} %get-tuple-element.53, bf16[128,128]{1,0:T(8,128)(2,1)S(1)} %get-tuple-element.68, bf16[128,128]{1,0:T(8,128)(2,1)S(1)} %collective-permute-done), kind=kOutput, calls=%fused_computation.112 | convolution fusion | flops 25231360 | bytes 294913 | tf_op jit(solution)/shard_map/transpose(jvp(tgn,sgn->gts))/dot_general | solution.py:47
  49.6 2.0 %copy.65 = f32[128,1024]{1,0:T(8,128)} copy(f32[128,1024]{0,1:T(8,128)} %bitcast.151) | data formatting | bytes 1048576 | tf_op jit(solution)/shard_map/transpose(jvp())/reshape | solution.py:54
  51.7 2.3 %fusion.12 = bf16[1,128,1024]{2,1,0:T(8,128)(2,1)} fusion(bf16[1,128,1024]{2,1,0:T(8,128)(2,1)} %param.19, f32[1,128,1024]{2,1,0:T(8,128)} %copy.72, bf16[1,128,1024]{2,1,0:T(8,128)(2,1)S(1)} %copy-done.4, f32[128]{0:T(128)} %copy-done.36, f32[128]{0:T(128)} %copy-done.48, f32[1024]{0:T(1024)S(1)} %copy-done.22, f32[128]{0:T(128)} %copy-done.30), kind=kLoop, calls=%fused_computation.19 | loop fusion | flops 2621440 | bytes 1316352 | tf_op jit(solution)/shard_map/convert_element_type | solution.py:384
  53.9 1.7 %multiply_reduce_fusion.5 = (f32[1024]{0:T(1024)S(1)}, f32[1024]{0:T(1024)S(1)}, f32[1024]{0:T(1024)S(1)}, f32[1024]{0:T(1024)S(1)}, f32[128,1024]{1,0:T(8,128)S(1)}) fusion(f32[128,1024]{1,0:T(8,128)S(1)} %bitcast_convert_fusion, bf16[1,128,1024]{2,1,0:T(8,128)(2,1)} %param.16, f32[128,1024]{1,0:T(8,128)} %get-tuple-element.71, f32[128,1024]{1,0:T(8,128)} %copy.65), kind=kLoop, calls=%fused_computation.53 | loop fusion | flops 2355200 | bytes 2375680 | tf_op jit(solution)/shard_map/transpose(jvp())/reduce_sum | solution.py:29
  56.3 2.4 %collective-permute-start.3 = (bf16[128,1024]{1,0:T(8,128)(2,1)}, bf16[128,1024]{1,0:T(8,128)(2,1)}, u32[]{:S(2)}, u32[]{:S(2)}) collective-permute-start(bf16[128,1024]{1,0:T(8,128)(2,1)} %get-tuple-element.77), channel_id=1, source_target_pairs={{0,4},{4,8},{8,12},{12,16},{16,20},{20,24},{24,28},{28,0},{1,5},{5... | collective-permute-start | bytes 786440 | tf_op jit(solution)/shard_map/ppermute | solution.py:312
  60.6 51.6 %shard_map.230 = (bf16[8,128,1280]{2,1,0:T(8,128)(2,1)S(1)}, f32[8,1024]{1,0:T(8,128)S(1)}, bf16[2,4,32,1024]{3,2,1,0:T(8,128)(2,1)S(1)}) custom-call(bf16[128,1280]{1,0:T(8,128)(2,1)S(1)} %concatenate.15.g_ref, bf16[1024,1280]{1,0:T(8,128)(2,1)S(1)} %concatenate.16.w_ref, f32[8,1024]{1,0:T(8,128)S(1)} %select_maximum_fusion.q_ref), custom_call_target="tpu_custom_call" | custom-call | flops 2684354560 | bytes 62914560 | tf_op jit(solution)/shard_map/pallas_call | solution.py:258
  117.8 4.8 %collective-permute-start.6 = (bf16[128,1024]{1,0:T(8,128)(2,1)S(1)}, bf16[128,1024]{1,0:T(8,128)(2,1)S(1)}, u32[]{:S(2)}, u32[]{:S(2)}) collective-permute-start(bf16[128,1024]{1,0:T(8,128)(2,1)S(1)} %copy-done.17), channel_id=1, source_target_pairs={{0,16},{4,20},{8,24},{12,28},{16,0},{20,4},{24,8},{28,12},{1,17},{... | collective-permute-start | bytes 786440 | tf_op jit(solution)/shard_map/ppermute | solution.py:312
  124.3 1.7 %constant_dynamic-update-slice_fusion.5 = bf16[1024,1024]{1,0:T(8,128)(2,1)} fusion(bf16[1024,1024]{1,0:T(8,128)(2,1)} %constant_dynamic-update-slice_fusion.6, bf16[128,1024]{1,0:T(8,128)(2,1)} %collective-permute-done.4), kind=kLoop, calls=%fused_computation.140 | loop fusion | bytes 524288
  125.9 1.7 %constant_dynamic-update-slice_fusion.4 = bf16[1024,1024]{1,0:T(8,128)(2,1)} fusion(bf16[1024,1024]{1,0:T(8,128)(2,1)} %constant_dynamic-update-slice_fusion.5, bf16[128,1024]{1,0:T(8,128)(2,1)} %collective-permute-done.5), kind=kLoop, calls=%fused_computation.139 | loop fusion | bytes 524288
  127.6 12.2 %collective-permute-done.6 = bf16[128,1024]{1,0:T(8,128)(2,1)S(1)} collective-permute-done((bf16[128,1024]{1,0:T(8,128)(2,1)S(1)}, bf16[128,1024]{1,0:T(8,128)(2,1)S(1)}, u32[]{:S(2)}, u32[]{:S(2)}) %collective-permute-start.6) | collective-permute-done | bytes 262176 | tf_op jit(solution)/shard_map/ppermute | solution.py:312
  140.5 1.7 %constant_dynamic-update-slice_fusion.2 = bf16[1024,1024]{1,0:T(8,128)(2,1)} fusion(bf16[1024,1024]{1,0:T(8,128)(2,1)} %constant_dynamic-update-slice_fusion.3, bf16[128,1024]{1,0:T(8,128)(2,1)} %collective-permute-done.7), kind=kLoop, calls=%fused_computation.137 | loop fusion | bytes 524288
  142.9 1.7 %constant_dynamic-update-slice_fusion = bf16[1024,1024]{1,0:T(8,128)(2,1)} fusion(bf16[1024,1024]{1,0:T(8,128)(2,1)} %constant_dynamic-update-slice_fusion.1, bf16[128,1024]{1,0:T(8,128)(2,1)} %collective-permute-done.9), kind=kLoop, calls=%fused_computation.135 | loop fusion | bytes 524288 | tf_op jit(solution)/shard_map/concatenate | solution.py:377
  144.5 4.6 %convolution_convert_fusion = bf16[1024,1280]{1,0:T(8,128)(2,1)S(1)} fusion(bf16[1024,1024]{1,0:T(8,128)(2,1)} %constant_dynamic-update-slice_fusion, bf16[1024,1280]{1,0:T(8,128)(2,1)S(1)} %bitcast.142), kind=kOutput, calls=%fused_computation | convolution fusion | flops 2685665280 | bytes 7340032 | tf_op jit(solution)/shard_map/dot_general | solution.py:376
  (183 shorter events, 34.4 us)
Async XLA Ops:
  0.6 10.1 %copy-start.53 = (f32[16]{0:T(128)S(1)}, f32[16]{0:T(128)}, u32[]{:S(2)}) copy-start(f32[16]{0:T(128)} %param.23) | copy-start | bytes 196
  0.7 10.1 %copy-start.27 = (f32[4,1024]{1,0:T(4,128)S(1)}, f32[4,1024]{1,0:T(4,128)}, u32[]{:S(2)}) copy-start(f32[4,1024]{1,0:T(4,128)} %param.20) | copy-start | bytes 49156
  0.7 10.2 %copy-start.31 = (f32[1,128,16]{1,2,0:T(8,128)S(1)}, f32[1,128,16]{1,2,0:T(8,128)}, u32[]{:S(2)}) copy-start(f32[1,128,16]{1,2,0:T(8,128)} %param.18) | copy-start | bytes 24580
  1.5 9.3 %copy-start.38 = (f32[128]{0:T(128)}, f32[128]{0:T(128)S(1)}, u32[]{:S(2)}) copy-start(f32[128]{0:T(128)S(1)} %get-tuple-element.97) | copy-start | bytes 1540
  1.5 9.3 %copy-start.40 = (f32[128]{0:T(128)}, f32[128]{0:T(128)S(1)}, u32[]{:S(2)}) copy-start(f32[128]{0:T(128)S(1)} %get-tuple-element.98) | copy-start | bytes 1540
  1.5 9.3 %copy-start.42 = (f32[128]{0:T(128)}, f32[128]{0:T(128)S(1)}, u32[]{:S(2)}) copy-start(f32[128]{0:T(128)S(1)} %get-tuple-element.99) | copy-start | bytes 1540
  1.5 9.3 %copy-start.44 = (f32[128]{0:T(128)}, f32[128]{0:T(128)S(1)}, u32[]{:S(2)}) copy-start(f32[128]{0:T(128)S(1)} %get-tuple-element.100) | copy-start | bytes 1540
  1.5 9.4 %copy-start.9 = (bf16[1,128,1024]{2,1,0:T(8,128)(2,1)S(1)}, bf16[1,128,1024]{2,1,0:T(8,128)(2,1)}, u32[]{:S(2)}) copy-start(bf16[1,128,1024]{2,1,0:T(8,128)(2,1)} %param.16) | copy-start | bytes 786436
  2.4 8.7 %copy-start.12 = (f32[128,128]{1,0:T(8,128)}, f32[128,128]{1,0:T(8,128)S(1)}, u32[]{:S(2)}) copy-start(f32[128,128]{1,0:T(8,128)S(1)} %bitcast_convert_fusion.1) | copy-start | bytes 196612
  3.0 10.1 %collective-permute-start = (bf16[128,128]{1,0:T(8,128)(2,1)S(1)}, bf16[128,128]{1,0:T(8,128)(2,1)S(1)}, u32[]{:S(2)}, u32[]{:S(2)}) collective-permute-start(bf16[128,128]{1,0:T(8,128)(2,1)S(1)} %get-tuple-element.68), channel_id=1, source_target_pairs={{0,1},{1,0},{2,3},{3,2},{4,5},{5,4},{6,7},{7,6},{8,9},{9,8},{10,11... | collective-permute-start | bytes 98312 | tf_op jit(solution)/shard_map/ppermute | solution.py:20
  3.7 7.3 %copy-start.46 = (f32[16]{0:T(128)S(1)}, f32[16]{0:T(128)}, u32[]{:S(2)}) copy-start(f32[16]{0:T(128)} %param.22) | copy-start | bytes 196
  6.4 6.3 %copy-start.5 = (bf16[1,128,1024]{2,1,0:T(8,128)(2,1)S(1)}, bf16[1,128,1024]{2,1,0:T(8,128)(2,1)}, u32[]{:S(2)}) copy-start(bf16[1,128,1024]{2,1,0:T(8,128)(2,1)} %param.19) | copy-start | bytes 786436
  6.4 136.5 %collective-permute-start.9 = (bf16[128,1024]{1,0:T(8,128)(2,1)}, bf16[128,1024]{1,0:T(8,128)(2,1)}, u32[]{:S(2)}, u32[]{:S(2)}) collective-permute-start(bf16[128,1024]{1,0:T(8,128)(2,1)} %get-tuple-element.72), channel_id=1, source_target_pairs={{0,28},{4,0},{8,4},{12,8},{16,12},{20,16},{24,20},{28,24},{1,29},{... | collective-permute-start | bytes 786440 | tf_op jit(solution)/shard_map/ppermute | solution.py:312
  6.7 133.8 %collective-permute-start.7 = (bf16[128,1024]{1,0:T(8,128)(2,1)}, bf16[128,1024]{1,0:T(8,128)(2,1)}, u32[]{:S(2)}, u32[]{:S(2)}) collective-permute-start(bf16[128,1024]{1,0:T(8,128)(2,1)} %get-tuple-element.73), channel_id=1, source_target_pairs={{0,20},{4,24},{8,28},{12,0},{16,4},{20,8},{24,12},{28,16},{1,21},{... | collective-permute-start | bytes 786440 | tf_op jit(solution)/shard_map/ppermute | solution.py:312
  7.7 118.3 %collective-permute-start.5 = (bf16[128,1024]{1,0:T(8,128)(2,1)}, bf16[128,1024]{1,0:T(8,128)(2,1)}, u32[]{:S(2)}, u32[]{:S(2)}) collective-permute-start(bf16[128,1024]{1,0:T(8,128)(2,1)} %get-tuple-element.75), channel_id=1, source_target_pairs={{0,12},{4,16},{8,20},{12,24},{16,28},{20,0},{24,4},{28,8},{1,13},{... | collective-permute-start | bytes 786440 | tf_op jit(solution)/shard_map/ppermute | solution.py:312
  9.9 114.3 %collective-permute-start.4 = (bf16[128,1024]{1,0:T(8,128)(2,1)}, bf16[128,1024]{1,0:T(8,128)(2,1)}, u32[]{:S(2)}, u32[]{:S(2)}) collective-permute-start(bf16[128,1024]{1,0:T(8,128)(2,1)} %get-tuple-element.76), channel_id=1, source_target_pairs={{0,8},{4,12},{8,16},{12,20},{16,24},{20,28},{24,0},{28,4},{1,9},{5... | collective-permute-start | bytes 786440 | tf_op jit(solution)/shard_map/ppermute | solution.py:312
  15.5 6.1 %copy-start.2 = (f32[128,16,64]{0,2,1:T(8,128)}, f32[128,16,64]{0,2,1:T(8,128)S(1)}, u32[]{:S(2)}) copy-start(f32[128,16,64]{0,2,1:T(8,128)S(1)} %get-tuple-element.104) | copy-start | bytes 1572868
  16.7 11.5 %collective-permute-start.1 = (f32[2,128]{1,0:T(2,128)}, f32[2,128]{1,0:T(2,128)}, u32[]{:S(2)}, u32[]{:S(2)}) collective-permute-start(f32[2,128]{1,0:T(2,128)} %pad_maximum_fusion), channel_id=1, source_target_pairs={{0,1},{1,0},{2,3},{3,2},{4,5},{5,4},{6,7},{7,6},{8,9},{9,8},{10,11... | collective-permute-start | bytes 3080 | tf_op jit(solution)/shard_map/ppermute | solution.py:20
  45.9 10.4 %collective-permute-start.2 = (bf16[128,128]{1,0:T(8,128)(2,1)}, bf16[128,128]{1,0:T(8,128)(2,1)S(1)}, u32[]{:S(2)}, u32[]{:S(2)}) collective-permute-start(bf16[128,128]{1,0:T(8,128)(2,1)} %get-tuple-element.105), channel_id=1, source_target_pairs={{0,1},{1,0},{2,3},{3,2},{4,5},{5,4},{6,7},{7,6},{8,9},{9,8},{10,11... | collective-permute-start | bytes 98312 | tf_op jit(solution)/shard_map/ppermute | solution.py:20
  56.3 61.5 %collective-permute-start.3 = (bf16[128,1024]{1,0:T(8,128)(2,1)}, bf16[128,1024]{1,0:T(8,128)(2,1)}, u32[]{:S(2)}, u32[]{:S(2)}) collective-permute-start(bf16[128,1024]{1,0:T(8,128)(2,1)} %get-tuple-element.77), channel_id=1, source_target_pairs={{0,4},{4,8},{8,12},{12,16},{16,20},{20,24},{24,28},{28,0},{1,5},{5... | collective-permute-start | bytes 786440 | tf_op jit(solution)/shard_map/ppermute | solution.py:312
  113.6 10.6 %copy-start.16 = (bf16[128,1024]{1,0:T(8,128)(2,1)S(1)}, bf16[128,1024]{1,0:T(8,128)(2,1)}, u32[]{:S(2)}) copy-start(bf16[128,1024]{1,0:T(8,128)(2,1)} %get-tuple-element.78) | copy-start | bytes 786436
  117.2 27.3 %copy-start.1 = (bf16[8,128,1280]{2,1,0:T(8,128)(2,1)S(1)}, bf16[8,128,1280]{2,1,0:T(8,128)(2,1)}, u32[]{:S(2)}) copy-start(bf16[8,128,1280]{2,1,0:T(8,128)(2,1)} %copy-done) | copy-start | bytes 7864324
  117.8 21.9 %collective-permute-start.6 = (bf16[128,1024]{1,0:T(8,128)(2,1)S(1)}, bf16[128,1024]{1,0:T(8,128)(2,1)S(1)}, u32[]{:S(2)}, u32[]{:S(2)}) collective-permute-start(bf16[128,1024]{1,0:T(8,128)(2,1)S(1)} %copy-done.17), channel_id=1, source_target_pairs={{0,16},{4,20},{8,24},{12,28},{16,0},{20,4},{24,8},{28,12},{1,17},{... | collective-permute-start | bytes 786440 | tf_op jit(solution)/shard_map/ppermute | solution.py:312
  124.2 17.9 %collective-permute-start.8 = (bf16[128,1024]{1,0:T(8,128)(2,1)S(1)}, bf16[128,1024]{1,0:T(8,128)(2,1)S(1)}, u32[]{:S(2)}, u32[]{:S(2)}) collective-permute-start(bf16[128,1024]{1,0:T(8,128)(2,1)S(1)} %copy-done.16), channel_id=1, source_target_pairs={{0,24},{4,28},{8,0},{12,4},{16,8},{20,12},{24,16},{28,20},{1,25},{... | collective-permute-start | bytes 786440 | tf_op jit(solution)/shard_map/ppermute | solution.py:312
  (40 other events, 130.5 us)

commit v3 on v2

--- a/solution.py
+++ b/solution.py
@@ -65,8 +65,19 @@
 
 
 def exchange_kernel(
-    n, m, g_ref, w_ref, q_ref, all_ref, sum_ref, out_ref,
-    part_buf, far_buf, red_buf, q_buf,
+    n, m, g_ref, wx_ref, wb_ref, wd_ref, q_ref, in_ref, *rest
+):
+    rows_refs = rest[: n - 1]
+    gwx_ref, gwb_ref, gwd_ref, sum_ref, out_ref = rest[n - 1 : n + 4]
+    exchange_steps(
+        n, m, g_ref, wx_ref, wb_ref, wd_ref, q_ref, in_ref, rows_refs,
+        gwx_ref, gwb_ref, gwd_ref, sum_ref, out_ref, *rest[n + 4 :])
+
+
+def exchange_steps(
+    n, m, g_ref, wx_ref, wb_ref, wd_ref, q_ref, in_ref, rows_refs,
+    gwx_ref, gwb_ref, gwd_ref, sum_ref, out_ref,
+    w_ref, all_ref, rows_buf, total_buf, rows_sem, part_buf, far_buf, red_buf, q_buf,
     ring_send, ring_recv, q_send, q_recv, far_send, far_recv, red_send, red_recv,
 ):
     d, t = lax.axis_index("dp"), lax.axis_index("tensor")
@@ -79,6 +90,22 @@
     right, left = ring_index(place + 1, n), ring_index(place - 1, n)
     right_steps = n // 2
     left_steps = n - 1 - right_steps
+    depth = wx_ref.shape[0]
+    cut_b = wx_ref.shape[1]
+    cut_d = cut_b + wb_ref.shape[1]
+    cut_end = cut_d + wd_ref.shape[1]
+    loads = []
+    for k in range(n):
+        spot = 0
+        source = in_ref.at[:, pl.ds(pl.multiple_of(d * depth, 128), depth)]
+        if k:
+            source = rows_refs[k - 1]
+            owner = lax.rem(d - k + n, n)
+            owner_place = jnp.where(lax.rem(owner, 2) == 0, owner // 2, n - 1 - owner // 2)
+            apart = lax.rem(place - owner_place + n, n)
+            spot = jnp.where(apart <= right_steps, 2 * apart - 1, 2 * (n - apart))
+        loads.append(pltpu.make_async_copy(source, rows_buf.at[spot], rows_sem.at[k]))
+        loads[-1].start()
     barrier = pltpu.get_barrier_semaphore()
 
     def signal(dp, tensor):
@@ -123,11 +150,11 @@
             device_id={"dp": lax.rem(d + k, n)}, device_id_type=pl.DeviceIdType.MESH)
 
     def ring_copy(way, k):
-        source = ring_index(place - k if way == 0 else place + k, n)
         target = right if way == 0 else left
+        held = 2 * k - 1 if way == 0 else 2 * k
         return pltpu.make_async_remote_copy(
-            src_ref=all_ref.at[lax.rem(d - source + n, n)],
-            dst_ref=all_ref.at[lax.rem(target - source + n, n)],
+            src_ref=all_ref.at[jnp.maximum(held, 0)],
+            dst_ref=all_ref.at[held + 2],
             send_sem=ring_send.at[way, k], recv_sem=ring_recv.at[way, k],
             device_id={"dp": target}, device_id_type=pl.DeviceIdType.MESH)
 
@@ -159,6 +186,12 @@
         return c
 
     lax.fori_loop(1, n, q_start, 0)
+    w_ref[:, :cut_b] = wx_ref[...]
+    w_ref[:, cut_b:cut_d] = wb_ref[...]
+    w_ref[:, cut_d:] = jnp.zeros((depth, w_ref.shape[1] - cut_d), w_ref.dtype)
+    w_ref[:, cut_d:cut_end] = wd_ref[...]
+    for load in loads:
+        load.wait()
 
     def reduce(j):
         total = part_buf[j, t].astype(jnp.float32)
@@ -195,14 +228,31 @@
             def _():
                 ring_copy(1, k).start()
 
-        slot = lax.rem(d - source_of(j) + n, n)
         product = lax.dot_general(
-            all_ref[slot], w_ref[...], (((1,), (1,)), ((), ())),
+            all_ref[j], w_ref[...], (((1,), (1,)), ((), ())),
             preferred_element_type=jnp.float32)
         part_buf[j] = product.reshape(m, part, product.shape[1]).astype(jnp.bfloat16)
         for hop in range(1, m):
             far_copy(j, hop).start()
 
+        @pl.when(lax.rem(j, 2) == 1)
+        def _():
+            grads = all_ref[pl.ds(j - 1, 2)].reshape(2 * seq_len, all_ref.shape[2])
+            tile = min(256, depth)
+            for low in range(0, depth, tile):
+                block = rows_buf[pl.ds(j - 1, 2), :, low : low + tile]
+                term = lax.dot_general(
+                    block.reshape(2 * seq_len, tile), grads, (((0,), (0,)), ((), ())),
+                    preferred_element_type=jnp.float32)
+
+                @pl.when(j == 1)
+                def _():
+                    total_buf[low : low + tile] = term
+
+                @pl.when(j > 1)
+                def _():
+                    total_buf[low : low + tile] += term
+
         @pl.when(j > 0)
         def _():
             reduce(j - 1)
@@ -216,6 +266,9 @@
         return c
 
     lax.fori_loop(1, n, q_finish, 0)
+    gwx_ref[...] = total_buf[:, :cut_b].astype(jnp.bfloat16)
+    gwb_ref[...] = total_buf[:, cut_b:cut_d].astype(jnp.bfloat16)
+    gwd_ref[...] = total_buf[:, cut_d:cut_end].astype(jnp.bfloat16)
     sum_ref[...] = jnp.sum(q_buf[...], axis=0)
     for k in range(right_steps):
         ring_copy(0, k).wait_send()
@@ -249,34 +302,39 @@
     lax.fori_loop(0, ratio * m, arrive, 0)
 
 
-def exchange(g_cat, w_cat, packed, n, m):
+def exchange(g_cat, weights, packed, inputs, rows, n, m):
     seq_len, width = g_cat.shape
-    rows = w_cat.shape[0]
+    depth = weights[0].shape[0]
     part = seq_len // m
     vmem = pl.BlockSpec(memory_space=pltpu.VMEM)
     dma = pltpu.SemaphoreType.DMA
     return pl.pallas_call(
         functools.partial(exchange_kernel, n, m),
         out_shape=(
-            jax.ShapeDtypeStruct((n, seq_len, width), jnp.bfloat16),
+            *(jax.ShapeDtypeStruct(w.shape, jnp.bfloat16) for w in weights),
             jax.ShapeDtypeStruct(packed.shape, jnp.float32),
-            jax.ShapeDtypeStruct((n // m, m, part, rows), jnp.bfloat16),
+            jax.ShapeDtypeStruct((n // m, m, part, depth), jnp.bfloat16),
         ),
-        in_specs=[vmem] * 3,
-        out_specs=[vmem] * 3,
+        in_specs=[vmem] * 5 + [pl.BlockSpec(memory_space=pl.ANY)] * n,
+        out_specs=[vmem] * 5,
         scratch_shapes=[
-            pltpu.VMEM((n, m, part, rows), jnp.bfloat16),
-            pltpu.VMEM((n, m, part, rows), jnp.bfloat16),
-            pltpu.VMEM((n, part, rows), jnp.bfloat16),
+            pltpu.VMEM((depth, width), jnp.bfloat16),
+            pltpu.VMEM((n, seq_len, width), jnp.bfloat16),
+            pltpu.VMEM((n, seq_len, depth), jnp.bfloat16),
+            pltpu.VMEM((depth, width), jnp.float32),
+            dma((n,)),
+            pltpu.VMEM((n, m, part, depth), jnp.bfloat16),
+            pltpu.VMEM((n, m, part, depth), jnp.bfloat16),
+            pltpu.VMEM((n, part, depth), jnp.bfloat16),
             pltpu.VMEM((n,) + packed.shape, jnp.float32),
             dma((2, n)), dma((2, n)), dma((n,)), dma((n,)),
             dma((n, m)), dma((n, m)), dma((n,)), dma((n // m, m)),
         ],
         compiler_params=pltpu.CompilerParams(
-            collective_id=0, has_side_effects=True, vmem_limit_bytes=40 * 2**20),
+            collective_id=0, has_side_effects=True, vmem_limit_bytes=58 * 2**20),
         cost_estimate=pl.CostEstimate(
-            flops=2 * n * seq_len * width * rows, bytes_accessed=60 * 2**20, transcendentals=0),
-    )(g_cat, w_cat, packed)
+            flops=4 * n * seq_len * width * depth, bytes_accessed=60 * 2**20, transcendentals=0),
+    )(g_cat, *weights, packed, inputs, *rows)
 
 
 def body(
@@ -306,7 +364,7 @@
     def rows_of(owner):
         return lax.dynamic_slice_in_dim(inputs[0], owner * dp_rows, dp_rows, axis=1)
 
-    rows = [rows_of(here)]
+    rows = []
     for hop in range(1, dp_size):
         route = [(i, (i + hop) % dp_size) for i in range(dp_size)]
         rows.append(lax.ppermute(rows_of(lax.rem(here + hop, dp_size)), "dp", route))
@@ -359,8 +417,8 @@
          jnp.zeros((seq_len, pad), jnp.bfloat16)],
         axis=1,
     )
-    w_cat = jnp.concatenate([w_x, w_bc, w_dt, jnp.zeros((dp_rows, pad), jnp.bfloat16)], axis=1)
-    g_all, packed, moved = exchange(g_cat, w_cat, packed, dp_size, tensor_size)
+    grad_wx, grad_wbc, grad_wdt, packed, moved = exchange(
+        g_cat, (w_x, w_bc, w_dt), packed, inputs[0], rows, dp_size, tensor_size)
     taps = grad_cx.shape[0]
     flat = packed[taps + 1 :].reshape(-1)
     cut = taps * half_width
@@ -373,18 +431,12 @@
         packed[taps],
     )
     grad_in = moved.transpose(1, 2, 0, 3).reshape(1, seq_len, model // tensor_size)
-    grad_w = lax.dot_general(
-        jnp.concatenate(rows, axis=0),
-        g_all.reshape(dp_size * seq_len, width + pad),
-        (((0,), (0,)), ((), ())),
-        preferred_element_type=jnp.float32,
-    ).astype(jnp.bfloat16)[:, :width]
     return (
         grad_in,
         grad_z.astype(jnp.bfloat16)[None],
-        grad_w[:, :channels],
-        grad_w[:, channels : channels + half_width],
-        grad_w[:, channels + half_width :],
+        grad_wx,
+        grad_wbc,
+        grad_wdt,
         param_grads[0],
         param_grads[1],
         param_grads[2],

time: 153 us -> 138 us (0.902)
  the two profiles are of different devices: /device:TPU:27 before, /device:TPU:17 now
where the time goes in v3:
time: 138 us
  Pallas kernels  59.4 us (43%)
  waiting for transfers between devices  25.8 us (19%)
  local copies, waits for them, and re-layouts  22.9 us (17%)
  other arithmetic  11.9 us (9%)
  starting transfers between devices  9.12 us (7%)
  matrix products  7.37 us (5%)
    pallas_call x1, Pallas kernels, exchange(): pl.pallas_call(functools.partial(exchange_kernel, n, m), out_shape=(*(jax...  59.4 us
    ppermute x7, waiting for transfers between devices, body(): lax.ppermute(rows_of(lax.rem(here + hop, dp_size)), 'dp', route)  25.8 us
    unnamed x63, local copies, waits for them, and re-layouts  6.76 us
    ppermute x7, starting transfers between devices, body(): lax.ppermute(rows_of(lax.rem(here + hop, dp_size)), 'dp', route)  6.68 us
    dot_general x3, matrix products, state_mix(): jnp.einsum('hts,shp->thp', weights, heads_x, precision=PRECISE)  6.61 us
  transfers between devices with their start and end apart: 10, of which 4 were waited for; matrix products, arithmetic and copies ran while one was open for 18% of the time, Pallas kernels for 0%

profile of v3, /device:TPU:17, one launch (start us, length us, event | category | flops | bytes accessed | tf_op | source)
XLA Modules:
  0.0 137.7 jit_solution(14581973340118612475)
XLA Ops:
  5.4 1.0 bitcast_convert_fusion
  8.6 2.0 %multiply_reduce_fusion.7 = (f32[128]{0:T(128)S(1)}, f32[128,16,64]{0,2,1:T(8,128)S(1)}) fusion(f32[128,16,64]{0,2,1:T(8,128)S(1)} %bitcast.142, f32[128,16,64]{0,2,1:T(8,128)S(1)} %bitcast.139, f32[16]{0:T(128)S(1)} %copy-done.26, f32[16,128]{1,0:T(8,128)S(1)} %copy.61, f32[16,128]{1,0:T(8,128)S(1)} %copy.59, f32[128,128]{1,0:T(8,128)S(1)} %fusion.54, ...), kind=kOutput, calls=%fused_computation.55 | convolution fusion | flops 203554688 | bytes 1671744 | tf_op jit(solution)/shard_map/jvp(hts,shp->thp)/dot_general | solution.py:56
  11.7 2.7 %dynamic-slice_bitcast_fusion = (bf16[128,1024]{1,0:T(8,128)(2,1)}, bf16[128,1024]{1,0:T(8,128)(2,1)}, bf16[128,1024]{1,0:T(8,128)(2,1)}, bf16[128,1024]{1,0:T(8...) fusion(bf16[1,128,8192]{2,1,0:T(8,128)(2,1)} %param.15, ...), kind=kLoop, calls=%fused_computation.76 | loop fusion | bytes 3670044 | tf_op jit(solution)/shard_map/dynamic_slice | solution.py:365
  14.4 1.1 collective-permute-start.9
  15.5 3.2 %collective-permute-start.6 = (bf16[128,1024]{1,0:T(8,128)(2,1)}, bf16[128,1024]{1,0:T(8,128)(2,1)}, u32[]{:S(2)}, u32[]{:S(2)}) collective-permute-start(bf16[128,1024]{1,0:T(8,128)(2,1)} %get-tuple-element.78), channel_id=1, source_target_pairs={{0,16},{4,20},{8,24},{12,28},{16,0},{20,4},{24,8},{28,12},{1,17},{... | collective-permute-start | bytes 786440 | tf_op jit(solution)/shard_map/ppermute | solution.py:370
  18.7 2.4 %collective-permute-start.5 = (bf16[128,1024]{1,0:T(8,128)(2,1)}, bf16[128,1024]{1,0:T(8,128)(2,1)}, u32[]{:S(2)}, u32[]{:S(2)}) collective-permute-start(bf16[128,1024]{1,0:T(8,128)(2,1)} %get-tuple-element.79), channel_id=1, source_target_pairs={{0,12},{4,16},{8,20},{12,24},{16,28},{20,0},{24,4},{28,8},{1,13},{... | collective-permute-start | bytes 786440 | tf_op jit(solution)/shard_map/ppermute | solution.py:370
  23.5 2.3 %multiply_reduce_fusion.2 = (f32[16]{0:T(128)}, f32[128,16,64]{0,2,1:T(8,128)S(1)}) fusion(f32[128,16,64]{0,2,1:T(8,128)} %bitcast.140, f32[128]{0:T(128)S(1)} %get-tuple-element.106, f32[128]{0:T(128)S(1)} %multiply_multiply_fusion, f32[128,16,64]{0,2,1:T(8,128)S(1)} %get-tuple-element.108, f32[128,16,64]{0,2,1:T(8,128)} %bitcast.143, ...), kind=kLoop, calls=%fused_computation.49 | loop fusion | flops 1703920 | bytes 2627136 | tf_op jit(solution)/shard_map/transpose(jvp())/reduce_sum | solution.py:57
  25.7 2.5 %fusion.7 = (f32[16,128]{1,0:T(8,128)S(1)}, f32[16,128]{1,0:T(8,128)S(1)}, f32[16,128]{1,0:T(8,128)S(1)}, f32[128,128]{1,0:T(8,128)S(1)}) fusion(f32[16,128]{1,0:T(8,128)S(1)} %copy.61, f32[16,128]{1,0:T(8,128)S(1)} %copy.59, f32[128,128]{1,0:T(8,128)S(1)} %fusion.54, pred[128,128]{1,0:T(8,128)(4,1)S(1)} %iota_compare_fusion, ...), kind=kOutput, calls=%fused_computation.13 | convolution fusion | flops 204711936 | bytes 1236992 | tf_op jit(solution)/shard_map/transpose(jvp(hts,shp->thp))/dot_general | solution.py:56
  28.3 2.1 %fusion = f32[128,16,64]{0,2,1:T(8,128)} fusion(f32[128,16,64]{0,2,1:T(8,128)S(1)} %get-tuple-element.71, f32[16,128]{1,0:T(8,128)S(1)} %copy.61, f32[16,128]{1,0:T(8,128)S(1)} %copy.59, f32[128,128]{1,0:T(8,128)S(1)} %fusion.54, pred[128,128]{1,0:T(8,128)(4,1)S(1)} %iota_compare_fusion, f32[16]{0:T(128)S(1)} %copy-done.27), kind=kOutput, calls=%fused_computation.1 | convolution fusion | flops 202637312 | bytes 1146944 | tf_op jit(solution)/shard_map/transpose(jvp(hts,shp->thp))/dot_general | solution.py:56
  30.5 1.1 reduce_window_sum.23
  32.1 1.7 %collective-permute-start.2 = (bf16[128,128]{1,0:T(8,128)(2,1)S(1)}, bf16[128,128]{1,0:T(8,128)(2,1)S(1)}, u32[]{:S(2)}, u32[]{:S(2)}) collective-permute-start(bf16[128,128]{1,0:T(8,128)(2,1)S(1)} %get-tuple-element.109), channel_id=1, source_target_pairs={{0,1},{1,0},{2,3},{3,2},{4,5},{5,4},{6,7},{7,6},{8,9},{9,8},{10,11... | collective-permute-start | bytes 98312 | tf_op jit(solution)/shard_map/ppermute | solution.py:20
  34.0 1.2 copy.65
  35.3 1.8 %fusion.12 = bf16[1,128,1024]{2,1,0:T(8,128)(2,1)} fusion(bf16[1,128,1024]{2,1,0:T(8,128)(2,1)S(1)} %copy-done.1, f32[1,128,1024]{2,1,0:T(8,128)S(1)} %copy.72, bf16[1,128,1024]{2,1,0:T(8,128)(2,1)S(1)} %copy-done, f32[128]{0:T(128)S(1)} %get-tuple-element.106, f32[128]{0:T(128)} %copy-done.21, f32[1024]{0:T(1024)S(1)} %copy-done.12, ...), kind=kLoop, calls=%fused_computation.18 | loop fusion | flops 2621440 | bytes 1316352 | tf_op jit(solution)/shard_map/convert_element_type | solution.py:436
  38.8 10.3 %collective-permute-done.7.rest_4_ = bf16[128,1024]{1,0:T(8,128)(2,1)} collective-permute-done((bf16[128,1024]{1,0:T(8,128)(2,1)}, bf16[128,1024]{1,0:T(8,128)(2,1)}, u32[]{:S(2)}, u32[]{:S(2)}) %collective-permute-start.7) | collective-permute-done | bytes 262176 | tf_op jit(solution)/shard_map/ppermute | solution.py:370
  50.7 4.0 %collective-permute-done.6.rest_3_ = bf16[128,1024]{1,0:T(8,128)(2,1)} collective-permute-done((bf16[128,1024]{1,0:T(8,128)(2,1)}, bf16[128,1024]{1,0:T(8,128)(2,1)}, u32[]{:S(2)}, u32[]{:S(2)}) %collective-permute-start.6) | collective-permute-done | bytes 262176 | tf_op jit(solution)/shard_map/ppermute | solution.py:370
  54.8 9.0 %collective-permute-done.4.rest_1_ = bf16[128,1024]{1,0:T(8,128)(2,1)S(1)} collective-permute-done((bf16[128,1024]{1,0:T(8,128)(2,1)S(1)}, bf16[128,1024]{1,0:T(8,128)(2,1)S(1)}, u32[]{:S(2)}, u32[]{:S(2)}) %collective-permute-start.4) | collective-permute-done | bytes 262176 | tf_op jit(solution)/shard_map/ppermute | solution.py:370
  63.8 2.3 %collective-permute-done.3.rest_0_ = bf16[128,1024]{1,0:T(8,128)(2,1)S(1)} collective-permute-done((bf16[128,1024]{1,0:T(8,128)(2,1)S(1)}, bf16[128,1024]{1,0:T(8,128)(2,1)S(1)}, u32[]{:S(2)}, u32[]{:S(2)}) %collective-permute-start.3) | collective-permute-done | bytes 262176 | tf_op jit(solution)/shard_map/ppermute | solution.py:370
  66.9 59.4 %shard_map.230 = (bf16[1024,1024]{1,0:T(8,128)(2,1)}, bf16[1024,128]{1,0:T(8,128)(2,1)}, bf16[1024,16]{1,0:T(8,128)(2,1)}, f32[8,1024]{1,0:T(8,128)}, bf16[2,4,32,1024]{3,2,1,0:T(8,128)(2,1)}) custom-call(bf16[128,1280]{1,0:T(8,128)(2,1)} %concatenate.9.g_ref, bf16[1024,1024]{1,0:T(8,128)(2,1)} %wx_ref.1, bf16[1024,128]{1,0:T(8,128)(2,1)} %wb_ref.1, ...), custom_call_target="tpu_custom_call" | custom-call | flops 5368709120 | bytes 62914560 | tf_op jit(solution)/shard_map/pallas_call | solution.py:311
  126.4 1.5 %slice.109 = f32[1,1024]{1,0:T(1,128)} slice(f32[8,1024]{1,0:T(8,128)} %get-tuple-element.20), slice={[4:5], [0:1024]} | slice | bytes 8192 | tf_op jit(solution)/shard_map/slice | solution.py:431
  128.7 1.4 slice.102
  130.1 1.6 %copy.70 = bf16[4,32,2,1024]{3,2,1,0:T(2,128)(2,1)S(1)} copy(bf16[4,32,2,1024]{3,1,0,2:T(8,128)(2,1)} %bitcast.147) | data formatting | bytes 1048576 | tf_op jit(solution)/shard_map/transpose | solution.py:433
  131.7 1.2 reshape.246
  134.0 1.7 %copy.73 = bf16[1024,16]{0,1:T(8,128)(2,1)} copy(bf16[1024,16]{1,0:T(8,128)(2,1)} %get-tuple-element.47) | data formatting | bytes 65536
  135.7 1.3 copy.76
  (121 shorter events, 17.6 us)
Async XLA Ops:
  0.6 7.2 %copy-start.1 = (bf16[1,128,1024]{2,1,0:T(8,128)(2,1)S(1)}, bf16[1,128,1024]{2,1,0:T(8,128)(2,1)}, u32[]{:S(2)}) copy-start(bf16[1,128,1024]{2,1,0:T(8,128)(2,1)} %param.19) | copy-start | bytes 786436
  2.3 5.9 %collective-permute-start = (bf16[128,128]{1,0:T(8,128)(2,1)S(1)}, bf16[128,128]{1,0:T(8,128)(2,1)S(1)}, u32[]{:S(2)}, u32[]{:S(2)}) collective-permute-start(bf16[128,128]{1,0:T(8,128)(2,1)S(1)} %get-tuple-element.72), channel_id=1, source_target_pairs={{0,1},{1,0},{2,3},{3,2},{4,5},{5,4},{6,7},{7,6},{8,9},{9,8},{10,11... | collective-permute-start | bytes 98312 | tf_op jit(solution)/shard_map/ppermute | solution.py:20
  3.7 4.5 %copy-start.19 = (f32[16]{0:T(128)}, f32[16]{0:T(128)S(1)}, u32[]{:S(2)}) copy-start(f32[16]{0:T(128)S(1)} %exponential_negate_fusion) | copy-start | bytes 196
  8.0 2.6 %copy-start.5 = (f32[1,128,1024]{1,2,0:T(8,128)}, f32[1,128,1024]{1,2,0:T(8,128)S(1)}, u32[]{:S(2)}) copy-start(f32[1,128,1024]{1,2,0:T(8,128)S(1)} %copy.62) | copy-start | bytes 1572868
  11.7 10.4 %copy-start.13 = (bf16[1024,16]{0,1:T(8,128)(2,1)S(1)}, bf16[1024,16]{0,1:T(8,128)(2,1)}, u32[]{:S(2)}) copy-start(bf16[1024,16]{0,1:T(8,128)(2,1)} %param.29) | copy-start | bytes 98308
  11.7 11.4 %collective-permute-start.1 = (f32[2,128]{1,0:T(2,128)}, f32[2,128]{1,0:T(2,128)S(1)}, u32[]{:S(2)}, u32[]{:S(2)}) collective-permute-start(f32[2,128]{1,0:T(2,128)} %pad_maximum_fusion), channel_id=1, source_target_pairs={{0,1},{1,0},{2,3},{3,2},{4,5},{5,4},{6,7},{7,6},{8,9},{9,8},{10,11... | collective-permute-start | bytes 3080 | tf_op jit(solution)/shard_map/ppermute | solution.py:20
  14.4 24.2 %collective-permute-start.9 = (bf16[128,1024]{1,0:T(8,128)(2,1)}, bf16[128,1024]{1,0:T(8,128)(2,1)}, u32[]{:S(2)}, u32[]{:S(2)}) collective-permute-start(bf16[128,1024]{1,0:T(8,128)(2,1)} %get-tuple-element.76), channel_id=1, source_target_pairs={{0,28},{4,0},{8,4},{12,8},{16,12},{20,16},{24,20},{28,24},{1,29},{... | collective-permute-start | bytes 786440 | tf_op jit(solution)/shard_map/ppermute | solution.py:370
  15.5 33.6 %collective-permute-start.7 = (bf16[128,1024]{1,0:T(8,128)(2,1)}, bf16[128,1024]{1,0:T(8,128)(2,1)}, u32[]{:S(2)}, u32[]{:S(2)}) collective-permute-start(bf16[128,1024]{1,0:T(8,128)(2,1)} %get-tuple-element.77), channel_id=1, source_target_pairs={{0,20},{4,24},{8,28},{12,0},{16,4},{20,8},{24,12},{28,16},{1,21},{... | collective-permute-start | bytes 786440 | tf_op jit(solution)/shard_map/ppermute | solution.py:370
  15.5 39.2 %collective-permute-start.6 = (bf16[128,1024]{1,0:T(8,128)(2,1)}, bf16[128,1024]{1,0:T(8,128)(2,1)}, u32[]{:S(2)}, u32[]{:S(2)}) collective-permute-start(bf16[128,1024]{1,0:T(8,128)(2,1)} %get-tuple-element.78), channel_id=1, source_target_pairs={{0,16},{4,20},{8,24},{12,28},{16,0},{20,4},{24,8},{28,12},{1,17},{... | collective-permute-start | bytes 786440 | tf_op jit(solution)/shard_map/ppermute | solution.py:370
  18.7 36.0 %collective-permute-start.5 = (bf16[128,1024]{1,0:T(8,128)(2,1)}, bf16[128,1024]{1,0:T(8,128)(2,1)}, u32[]{:S(2)}, u32[]{:S(2)}) collective-permute-start(bf16[128,1024]{1,0:T(8,128)(2,1)} %get-tuple-element.79), channel_id=1, source_target_pairs={{0,12},{4,16},{8,20},{12,24},{16,28},{20,0},{24,4},{28,8},{1,13},{... | collective-permute-start | bytes 786440 | tf_op jit(solution)/shard_map/ppermute | solution.py:370
  23.2 2.6 %copy-start.4 = (f32[128,1024]{0,1:T(8,128)S(1)}, f32[128,1024]{0,1:T(8,128)}, u32[]{:S(2)}) copy-start(f32[128,1024]{0,1:T(8,128)} %copy-done.3) | copy-start | bytes 1572868
  23.2 2.5 %copy-start.21 = (f32[128]{0:T(128)}, f32[128]{0:T(128)S(1)}, u32[]{:S(2)}) copy-start(f32[128]{0:T(128)S(1)} %multiply_multiply_fusion) | copy-start | bytes 1540
  25.7 2.5 %copy-start.27 = (f32[16]{0:T(128)S(1)}, f32[16]{0:T(128)}, u32[]{:S(2)}) copy-start(f32[16]{0:T(128)} %param.24) | copy-start | bytes 196
  28.2 5.6 %copy-start.18 = (f32[16]{0:T(128)S(1)}, f32[16]{0:T(128)}, u32[]{:S(2)}) copy-start(f32[16]{0:T(128)} %param.22) | copy-start | bytes 196
  28.2 5.6 %copy-start.20 = (f32[16]{0:T(128)S(1)}, f32[16]{0:T(128)}, u32[]{:S(2)}) copy-start(f32[16]{0:T(128)} %copy-done.19) | copy-start | bytes 196
  28.3 5.7 %copy-start.28 = (f32[16]{0:T(128)S(1)}, f32[16]{0:T(128)}, u32[]{:S(2)}) copy-start(f32[16]{0:T(128)} %param.23) | copy-start | bytes 196
  30.4 6.7 %copy-start.6 = (bf16[1,128,1024]{2,1,0:T(8,128)(2,1)S(1)}, bf16[1,128,1024]{2,1,0:T(8,128)(2,1)}, u32[]{:S(2)}) copy-start(bf16[1,128,1024]{2,1,0:T(8,128)(2,1)} %param.16) | copy-start | bytes 786436
  32.1 6.0 %collective-permute-start.2 = (bf16[128,128]{1,0:T(8,128)(2,1)S(1)}, bf16[128,128]{1,0:T(8,128)(2,1)S(1)}, u32[]{:S(2)}, u32[]{:S(2)}) collective-permute-start(bf16[128,128]{1,0:T(8,128)(2,1)S(1)} %get-tuple-element.109), channel_id=1, source_target_pairs={{0,1},{1,0},{2,3},{3,2},{4,5},{5,4},{6,7},{7,6},{8,9},{9,8},{10,11... | collective-permute-start | bytes 98312 | tf_op jit(solution)/shard_map/ppermute | solution.py:20
  37.8 11.3 %copy-start.8 = (bf16[128,1024]{1,0:T(8,128)(2,1)S(1)}, bf16[128,1024]{1,0:T(8,128)(2,1)}, u32[]{:S(2)}) copy-start(bf16[128,1024]{1,0:T(8,128)(2,1)} %get-tuple-element.82) | copy-start | bytes 786436
  37.9 12.2 %copy-start.22 = (f32[16]{0:T(128)S(1)}, f32[16]{0:T(128)}, u32[]{:S(2)}) copy-start(f32[16]{0:T(128)} %get-tuple-element.70) | copy-start | bytes 196
  38.5 25.3 %collective-permute-start.4 = (bf16[128,1024]{1,0:T(8,128)(2,1)S(1)}, bf16[128,1024]{1,0:T(8,128)(2,1)S(1)}, u32[]{:S(2)}, u32[]{:S(2)}) collective-permute-start(bf16[128,1024]{1,0:T(8,128)(2,1)S(1)} %copy-done.10), channel_id=1, source_target_pairs={{0,8},{4,12},{8,16},{12,20},{16,24},{20,28},{24,0},{28,4},{1,9},{5... | collective-permute-start | bytes 786440 | tf_op jit(solution)/shard_map/ppermute | solution.py:370
  38.8 27.3 %collective-permute-start.3 = (bf16[128,1024]{1,0:T(8,128)(2,1)S(1)}, bf16[128,1024]{1,0:T(8,128)(2,1)S(1)}, u32[]{:S(2)}, u32[]{:S(2)}) collective-permute-start(bf16[128,1024]{1,0:T(8,128)(2,1)S(1)} %copy-done.9), channel_id=1, source_target_pairs={{0,4},{4,8},{8,12},{12,16},{16,20},{20,24},{24,28},{28,0},{1,5},{5... | collective-permute-start | bytes 786440 | tf_op jit(solution)/shard_map/ppermute | solution.py:370
  49.2 17.0 %collective-permute-start.8 = (bf16[128,1024]{1,0:T(8,128)(2,1)S(1)}, bf16[128,1024]{1,0:T(8,128)(2,1)S(1)}, u32[]{:S(2)}, u32[]{:S(2)}) collective-permute-start(bf16[128,1024]{1,0:T(8,128)(2,1)S(1)} %copy-done.8), channel_id=1, source_target_pairs={{0,24},{4,28},{8,0},{12,4},{16,8},{20,12},{24,16},{28,20},{1,25},{... | collective-permute-start | bytes 786440 | tf_op jit(solution)/shard_map/ppermute | solution.py:370
  126.4 9.3 %copy-start.2 = (bf16[1024,1024]{1,0:T(8,128)(2,1)S(1)}, bf16[1024,1024]{1,0:T(8,128)(2,1)}, u32[]{:S(2)}) copy-start(bf16[1024,1024]{1,0:T(8,128)(2,1)} %get-tuple-element.127) | copy-start | bytes 6291460
  (15 other events, 20.2 us)

commit v4 on v3

--- a/solution.py
+++ b/solution.py
@@ -67,17 +67,16 @@
 def exchange_kernel(
     n, m, g_ref, wx_ref, wb_ref, wd_ref, q_ref, in_ref, *rest
 ):
-    rows_refs = rest[: n - 1]
-    gwx_ref, gwb_ref, gwd_ref, sum_ref, out_ref = rest[n - 1 : n + 4]
+    gwx_ref, gwb_ref, gwd_ref, sum_ref, out_ref = rest[:5]
     exchange_steps(
-        n, m, g_ref, wx_ref, wb_ref, wd_ref, q_ref, in_ref, rows_refs,
-        gwx_ref, gwb_ref, gwd_ref, sum_ref, out_ref, *rest[n + 4 :])
+        n, m, g_ref, wx_ref, wb_ref, wd_ref, q_ref, in_ref,
+        gwx_ref, gwb_ref, gwd_ref, sum_ref, out_ref, *rest[5:])
 
 
 def exchange_steps(
-    n, m, g_ref, wx_ref, wb_ref, wd_ref, q_ref, in_ref, rows_refs,
+    n, m, g_ref, wx_ref, wb_ref, wd_ref, q_ref, in_ref,
     gwx_ref, gwb_ref, gwd_ref, sum_ref, out_ref,
-    w_ref, all_ref, rows_buf, total_buf, rows_sem, part_buf, far_buf, red_buf, q_buf,
+    w_ref, all_ref, rows_buf, total_buf, rows_send, rows_recv, part_buf, far_buf, red_buf, q_buf,
     ring_send, ring_recv, q_send, q_recv, far_send, far_recv, red_send, red_recv,
 ):
     d, t = lax.axis_index("dp"), lax.axis_index("tensor")
@@ -94,18 +93,9 @@
     cut_b = wx_ref.shape[1]
     cut_d = cut_b + wb_ref.shape[1]
     cut_end = cut_d + wd_ref.shape[1]
-    loads = []
-    for k in range(n):
-        spot = 0
-        source = in_ref.at[:, pl.ds(pl.multiple_of(d * depth, 128), depth)]
-        if k:
-            source = rows_refs[k - 1]
-            owner = lax.rem(d - k + n, n)
-            owner_place = jnp.where(lax.rem(owner, 2) == 0, owner // 2, n - 1 - owner // 2)
-            apart = lax.rem(place - owner_place + n, n)
-            spot = jnp.where(apart <= right_steps, 2 * apart - 1, 2 * (n - apart))
-        loads.append(pltpu.make_async_copy(source, rows_buf.at[spot], rows_sem.at[k]))
-        loads[-1].start()
+    own_rows = pltpu.make_async_copy(
+        in_ref.at[:, pl.ds(pl.multiple_of(d * depth, 128), depth)], rows_buf.at[0], rows_recv.at[0])
+    own_rows.start()
     barrier = pltpu.get_barrier_semaphore()
 
     def signal(dp, tensor):
@@ -190,8 +180,23 @@
     w_ref[:, cut_b:cut_d] = wb_ref[...]
     w_ref[:, cut_d:] = jnp.zeros((depth, w_ref.shape[1] - cut_d), w_ref.dtype)
     w_ref[:, cut_d:cut_end] = wd_ref[...]
-    for load in loads:
-        load.wait()
+    own_rows.wait()
+
+    def rows_copy(k):
+        target = lax.rem(d + k, n)
+        target_place = jnp.where(lax.rem(target, 2) == 0, target // 2, n - 1 - target // 2)
+        apart = lax.rem(target_place - place + n, n)
+        spot = jnp.where(apart <= right_steps, 2 * apart - 1, 2 * (n - apart))
+        return pltpu.make_async_remote_copy(
+            src_ref=in_ref.at[:, pl.ds(pl.multiple_of(target * depth, 128), depth)],
+            dst_ref=rows_buf.at[spot], send_sem=rows_send.at[k], recv_sem=rows_recv.at[spot],
+            device_id={"dp": target}, device_id_type=pl.DeviceIdType.MESH)
+
+    def rows_wait(j):
+        pltpu.make_async_remote_copy(
+            src_ref=rows_buf.at[0], dst_ref=rows_buf.at[j],
+            send_sem=rows_send.at[0], recv_sem=rows_recv.at[j],
+            device_id={"dp": right}, device_id_type=pl.DeviceIdType.MESH).wait_recv()
 
     def reduce(j):
         total = part_buf[j, t].astype(jnp.float32)
@@ -235,23 +240,9 @@
         for hop in range(1, m):
             far_copy(j, hop).start()
 
-        @pl.when(lax.rem(j, 2) == 1)
-        def _():
-            grads = all_ref[pl.ds(j - 1, 2)].reshape(2 * seq_len, all_ref.shape[2])
-            tile = min(256, depth)
-            for low in range(0, depth, tile):
-                block = rows_buf[pl.ds(j - 1, 2), :, low : low + tile]
-                term = lax.dot_general(
-                    block.reshape(2 * seq_len, tile), grads, (((0,), (0,)), ((), ())),
-                    preferred_element_type=jnp.float32)
-
-                @pl.when(j == 1)
-                def _():
-                    total_buf[low : low + tile] = term
-
-                @pl.when(j > 1)
-                def _():
-                    total_buf[low : low + tile] += term
+        @pl.when(j < n - 1)
+        def _():
+            rows_copy(j + 1).start()
 
         @pl.when(j > 0)
         def _():
@@ -260,6 +251,33 @@
 
     lax.fori_loop(0, n, step, 0)
     reduce(n - 1)
+
+    def weight_pair(i, c):
+        j = 2 * i + 1
+
+        @pl.when(i > 0)
+        def _():
+            rows_wait(j - 1)
+
+        rows_wait(j)
+        grads = all_ref[pl.ds(j - 1, 2)].reshape(2 * seq_len, all_ref.shape[2])
+        tile = min(256, depth)
+        for low in range(0, depth, tile):
+            block = rows_buf[pl.ds(j - 1, 2), :, low : low + tile]
+            term = lax.dot_general(
+                block.reshape(2 * seq_len, tile), grads, (((0,), (0,)), ((), ())),
+                preferred_element_type=jnp.float32)
+
+            @pl.when(j == 1)
+            def _():
+                total_buf[low : low + tile] = term
+
+            @pl.when(j > 1)
+            def _():
+                total_buf[low : low + tile] += term
+        return c
+
+    lax.fori_loop(0, n // 2, weight_pair, 0)
 
     def q_finish(k, c):
         q_copy(k).wait()
@@ -270,6 +288,8 @@
     gwb_ref[...] = total_buf[:, cut_b:cut_d].astype(jnp.bfloat16)
     gwd_ref[...] = total_buf[:, cut_d:cut_end].astype(jnp.bfloat16)
     sum_ref[...] = jnp.sum(q_buf[...], axis=0)
+    for k in range(1, n):
+        rows_copy(k).wait_send()
     for k in range(right_steps):
         ring_copy(0, k).wait_send()
     for k in range(left_steps):
@@ -302,7 +322,7 @@
     lax.fori_loop(0, ratio * m, arrive, 0)
 
 
-def exchange(g_cat, weights, packed, inputs, rows, n, m):
+def exchange(g_cat, weights, packed, inputs, n, m):
     seq_len, width = g_cat.shape
     depth = weights[0].shape[0]
     part = seq_len // m
@@ -315,13 +335,14 @@
             jax.ShapeDtypeStruct(packed.shape, jnp.float32),
             jax.ShapeDtypeStruct((n // m, m, part, depth), jnp.bfloat16),
         ),
-        in_specs=[vmem] * 5 + [pl.BlockSpec(memory_space=pl.ANY)] * n,
+        in_specs=[vmem] * 5 + [pl.BlockSpec(memory_space=pl.ANY)],
         out_specs=[vmem] * 5,
         scratch_shapes=[
             pltpu.VMEM((depth, width), jnp.bfloat16),
             pltpu.VMEM((n, seq_len, width), jnp.bfloat16),
             pltpu.VMEM((n, seq_len, depth), jnp.bfloat16),
             pltpu.VMEM((depth, width), jnp.float32),
+            dma((n,)),
             dma((n,)),
             pltpu.VMEM((n, m, part, depth), jnp.bfloat16),
             pltpu.VMEM((n, m, part, depth), jnp.bfloat16),
@@ -334,7 +355,7 @@
             collective_id=0, has_side_effects=True, vmem_limit_bytes=58 * 2**20),
         cost_estimate=pl.CostEstimate(
             flops=4 * n * seq_len * width * depth, bytes_accessed=60 * 2**20, transcendentals=0),
-    )(g_cat, *weights, packed, inputs, *rows)
+    )(g_cat, *weights, packed, inputs)
 
 
 def body(
@@ -358,16 +379,6 @@
     half_width = bc_pre.shape[2]
     seq_len, model = inputs.shape[1:]
     dp_size, tensor_size = lax.axis_size("dp"), lax.axis_size("tensor")
-    dp_rows = model // dp_size
-    here = lax.axis_index("dp")
-
-    def rows_of(owner):
-        return lax.dynamic_slice_in_dim(inputs[0], owner * dp_rows, dp_rows, axis=1)
-
-    rows = []
-    for hop in range(1, dp_size):
-        route = [(i, (i + hop) % dp_size) for i in range(dp_size)]
-        rows.append(lax.ppermute(rows_of(lax.rem(here + hop, dp_size)), "dp", route))
     is_even = lax.axis_index("tensor") % 2 == 0
     bc_pre32 = bc_pre[0].astype(jnp.float32)
     own_half = state_act(bc_pre32, conv_bc).astype(jnp.bfloat16)
@@ -418,7 +429,7 @@
         axis=1,
     )
     grad_wx, grad_wbc, grad_wdt, packed, moved = exchange(
-        g_cat, (w_x, w_bc, w_dt), packed, inputs[0], rows, dp_size, tensor_size)
+        g_cat, (w_x, w_bc, w_dt), packed, inputs[0], dp_size, tensor_size)
     taps = grad_cx.shape[0]
     flat = packed[taps + 1 :].reshape(-1)
     cut = taps * half_width

time: 138 us -> 153 us (1.11)
  Pallas kernels: 59.4 us -> 111 us
  waiting for transfers between devices: 25.8 us -> 0.01 us
  starting transfers between devices: 9.12 us -> 1.32 us
  local copies, waits for them, and re-layouts: 22.9 us -> 19.9 us
    pallas_call x1, Pallas kernels: 59.4 us -> 111 us  [exchange(): pl.pallas_call(functools.partial(exchange_kernel, n, m), out_shape=(*(jax...]
    ppermute x7 -> x0, waiting for transfers between devices: 25.8 us -> none  [body(): lax.ppermute(rows_of(lax.rem(here + hop, dp_size)), 'dp', route)]
    ppermute x7 -> x0, starting transfers between devices: 6.68 us -> none  [body(): lax.ppermute(rows_of(lax.rem(here + hop, dp_size)), 'dp', route)]
    dynamic_slice x1 -> x0, local copies, waits for them, and re-layouts: 2.69 us -> none  [rows_of(): return lax.dynamic_slice_in_dim(inputs[0], owner * dp_rows, dp_rows, axis=1)]
    unnamed x63 -> x49, local copies, waits for them, and re-layouts: 6.76 us -> 5.65 us
  transfers between devices with their start and end apart: 10 -> 3, of which waited for: 4 -> 0; matrix products, arithmetic and copies ran while one was open for 18% -> 7% of each run, Pallas kernels for 0% -> 0%
where the time goes in v4:
time: 153 us; the launch traced here: 152 us
  Pallas kernels  111 us (73%)
  local copies, waits for them, and re-layouts  19.9 us (13%)
  other arithmetic  10.8 us (7%)
  matrix products  8.49 us (6%)
    pallas_call x1, Pallas kernels, exchange(): pl.pallas_call(functools.partial(exchange_kernel, n, m), out_shape=(*(jax...  111 us
    dot_general x3, matrix products, state_mix(): jnp.einsum('hts,shp->thp', weights, heads_x, precision=PRECISE)  7.73 us
    unnamed x49, local copies, waits for them, and re-layouts  5.65 us
  transfers between devices with their start and end apart: 3, of which 0 were waited for; matrix products, arithmetic and copies ran while one was open for 7% of the time, Pallas kernels for 0%

profile of v4, /device:TPU:17, one launch (start us, length us, event | category | flops | bytes accessed | tf_op | source)
XLA Modules:
  0.0 152.3 jit_solution(12885581842392406443)
XLA Ops:
  0.7 0.8 slice_bitcast_fusion.4
  1.5 0.8 bitcast_convert_fusion.1
  3.7 0.9 fusion.66
  4.6 0.8 copy.58
  5.4 1.0 bitcast_convert_fusion
  7.8 1.0 copy.62
  9.3 3.1 %multiply_reduce_fusion.7 = (f32[128]{0:T(128)S(1)}, f32[128,16,64]{0,2,1:T(8,128)S(1)}) fusion(f32[128,16,64]{0,2,1:T(8,128)} %bitcast.128, f32[128,16,64]{0,2,1:T(8,128)S(1)} %bitcast.125, f32[16]{0:T(128)S(1)} %copy-done.19, f32[16,128]{1,0:T(8,128)S(1)} %copy.61, f32[16,128]{1,0:T(8,128)S(1)} %copy.59, f32[128,128]{1,0:T(8,128)S(1)} %fusion.54, ...), kind=kOutput, calls=%fused_computation.55 | convolution fusion | flops 203554688 | bytes 1671744 | tf_op jit(solution)/shard_map/jvp(hts,shp->thp)/dot_general | solution.py:56
  13.6 0.9 copy.64
  14.5 0.8 copy.69.wd_ref
  15.9 1.8 %multiply_reduce_fusion.2 = (f32[16]{0:T(128)S(1)}, f32[128,16,64]{0,2,1:T(8,128)S(1)}) fusion(f32[128,16,64]{0,2,1:T(8,128)} %bitcast.126, f32[128]{0:T(128)S(1)} %get-tuple-element.99, f32[128]{0:T(128)S(1)} %multiply_multiply_fusion, f32[128,16,64]{0,2,1:T(8,128)S(1)} %get-tuple-element.101, f32[128,16,64]{0,2,1:T(8,128)} %bitcast.129, ...), kind=kLoop, calls=%fused_computation.49 | loop fusion | flops 1703920 | bytes 2627136 | tf_op jit(solution)/shard_map/transpose(jvp())/reduce_sum | solution.py:57
  17.7 2.5 %fusion.7 = (f32[16,128]{1,0:T(8,128)S(1)}, f32[16,128]{1,0:T(8,128)S(1)}, f32[16,128]{1,0:T(8,128)S(1)}, f32[128,128]{1,0:T(8,128)S(1)}) fusion(f32[16,128]{1,0:T(8,128)S(1)} %copy.61, f32[16,128]{1,0:T(8,128)S(1)} %copy.59, f32[128,128]{1,0:T(8,128)S(1)} %fusion.54, pred[128,128]{1,0:T(8,128)(4,1)S(1)} %iota_compare_fusion, ...), kind=kOutput, calls=%fused_computation.13 | convolution fusion | flops 204711936 | bytes 1236992 | tf_op jit(solution)/shard_map/transpose(jvp(hts,shp->thp))/dot_general | solution.py:56
  20.3 2.1 %fusion = f32[128,16,64]{0,2,1:T(8,128)} fusion(f32[128,16,64]{0,2,1:T(8,128)S(1)} %get-tuple-element.71, f32[16,128]{1,0:T(8,128)S(1)} %copy.61, f32[16,128]{1,0:T(8,128)S(1)} %copy.59, f32[128,128]{1,0:T(8,128)S(1)} %fusion.54, pred[128,128]{1,0:T(8,128)(4,1)S(1)} %iota_compare_fusion, f32[16]{0:T(128)S(1)} %copy-done.20), kind=kOutput, calls=%fused_computation.1 | convolution fusion | flops 202637312 | bytes 1146944 | tf_op jit(solution)/shard_map/transpose(jvp(hts,shp->thp))/dot_general | solution.py:56
  22.5 1.1 reduce_window_sum.23
  24.9 1.2 copy.65
  26.1 1.1 fusion.12
  29.4 0.8 concatenate.9.g_ref
  30.2 110.7 %shard_map.230 = (bf16[1024,1024]{1,0:T(8,128)(2,1)}, bf16[1024,128]{1,0:T(8,128)(2,1)}, bf16[1024,16]{1,0:T(8,128)(2,1)}, f32[8,1024]{1,0:T(8,128)}, bf16[2,4,32,1024]{3,2,1,0:T(8,128)(2,1)}) custom-call(bf16[128,1280]{1,0:T(8,128)(2,1)} %concatenate.9.g_ref, bf16[1024,1024]{1,0:T(8,128)(2,1)} %wx_ref.1, bf16[1024,128]{1,0:T(8,128)(2,1)} %wb_ref.1, ...), custom_call_target="tpu_custom_call" | custom-call | flops 5368709120 | bytes 62914560 | tf_op jit(solution)/shard_map/pallas_call | solution.py:331
  141.0 1.5 slice.109
  142.5 0.8 slice.103
  143.2 1.4 slice.102
  144.6 1.6 %copy.70 = bf16[4,32,2,1024]{3,2,1,0:T(2,128)(2,1)S(1)} copy(bf16[4,32,2,1024]{3,1,0,2:T(8,128)(2,1)} %bitcast.132) | data formatting | bytes 1048576 | tf_op jit(solution)/shard_map/transpose | solution.py:444
  146.2 1.2 reshape.239
  148.6 1.7 %copy.73 = bf16[1024,16]{0,1:T(8,128)(2,1)} copy(bf16[1024,16]{1,0:T(8,128)(2,1)} %get-tuple-element.47) | data formatting | bytes 65536
  150.3 1.3 copy.76
  (92 shorter events, 10.2 us)
Async XLA Ops:
  0.6 7.2 %copy-start.1 = (bf16[1,128,1024]{2,1,0:T(8,128)(2,1)S(1)}, bf16[1,128,1024]{2,1,0:T(8,128)(2,1)}, u32[]{:S(2)}) copy-start(bf16[1,128,1024]{2,1,0:T(8,128)(2,1)} %param.19) | copy-start | bytes 786436
  1.5 1.6 %copy-start.12 = (f32[128]{0:T(128)}, f32[128]{0:T(128)S(1)}, u32[]{:S(2)}) copy-start(f32[128]{0:T(128)S(1)} %get-tuple-element.97) | copy-start | bytes 1540
  1.5 7.5 %copy-start.10 = (f32[128]{0:T(128)}, f32[128]{0:T(128)S(1)}, u32[]{:S(2)}) copy-start(f32[128]{0:T(128)S(1)} %get-tuple-element.96) | copy-start | bytes 1540
  2.3 6.7 %collective-permute-start = (bf16[128,128]{1,0:T(8,128)(2,1)S(1)}, bf16[128,128]{1,0:T(8,128)(2,1)S(1)}, u32[]{:S(2)}, u32[]{:S(2)}) collective-permute-start(bf16[128,128]{1,0:T(8,128)(2,1)S(1)} %get-tuple-element.72), channel_id=1, source_target_pairs={{0,1},{1,0},{2,3},{3,2},{4,5},{5,4},{6,7},{7,6},{8,9},{9,8},{10,11... | collective-permute-start | bytes 98312 | tf_op jit(solution)/shard_map/ppermute | solution.py:20
  3.7 5.2 %copy-start.15 = (f32[16]{0:T(128)}, f32[16]{0:T(128)S(1)}, u32[]{:S(2)}) copy-start(f32[16]{0:T(128)S(1)} %exponential_negate_fusion) | copy-start | bytes 196
  6.4 2.9 %copy-start.19 = (f32[16]{0:T(128)S(1)}, f32[16]{0:T(128)}, u32[]{:S(2)}) copy-start(f32[16]{0:T(128)} %param.24) | copy-start | bytes 196
  9.0 3.4 %copy-start.3 = (f32[128,1024]{0,1:T(8,128)}, f32[128,1024]{0,1:T(8,128)S(1)}, u32[]{:S(2)}) copy-start(f32[128,1024]{0,1:T(8,128)S(1)} %copy.57) | copy-start | bytes 1572868
  9.3 3.4 %copy-start = (bf16[1,128,1024]{2,1,0:T(8,128)(2,1)S(1)}, bf16[1,128,1024]{2,1,0:T(8,128)(2,1)}, u32[]{:S(2)}) copy-start(bf16[1,128,1024]{2,1,0:T(8,128)(2,1)} %param.26) | copy-start | bytes 786436
  9.3 3.4 %copy-start.8 = (f32[1024]{0:T(1024)S(1)}, f32[1024]{0:T(1024)}, u32[]{:S(2)}) copy-start(f32[1024]{0:T(1024)} %param.25) | copy-start | bytes 12292
  12.4 2.1 %copy-start.9 = (bf16[1024,16]{0,1:T(8,128)(2,1)S(1)}, bf16[1024,16]{0,1:T(8,128)(2,1)}, u32[]{:S(2)}) copy-start(bf16[1024,16]{0,1:T(8,128)(2,1)} %param.29) | copy-start | bytes 98308
  13.5 2.1 %collective-permute-start.1 = (f32[2,128]{1,0:T(2,128)}, f32[2,128]{1,0:T(2,128)S(1)}, u32[]{:S(2)}, u32[]{:S(2)}) collective-permute-start(f32[2,128]{1,0:T(2,128)} %pad_maximum_fusion), channel_id=1, source_target_pairs={{0,1},{1,0},{2,3},{3,2},{4,5},{5,4},{6,7},{7,6},{8,9},{9,8},{10,11... | collective-permute-start | bytes 3080 | tf_op jit(solution)/shard_map/ppermute | solution.py:20
  15.6 2.1 %copy-start.4 = (f32[128,1024]{0,1:T(8,128)S(1)}, f32[128,1024]{0,1:T(8,128)}, u32[]{:S(2)}) copy-start(f32[128,1024]{0,1:T(8,128)} %copy-done.3) | copy-start | bytes 1572868
  15.6 2.0 %copy-start.17 = (f32[128]{0:T(128)}, f32[128]{0:T(128)S(1)}, u32[]{:S(2)}) copy-start(f32[128]{0:T(128)S(1)} %multiply_multiply_fusion) | copy-start | bytes 1540
  17.7 2.5 %copy-start.20 = (f32[16]{0:T(128)S(1)}, f32[16]{0:T(128)}, u32[]{:S(2)}) copy-start(f32[16]{0:T(128)} %param.24) | copy-start | bytes 196
  20.2 4.5 %copy-start.14 = (f32[16]{0:T(128)S(1)}, f32[16]{0:T(128)}, u32[]{:S(2)}) copy-start(f32[16]{0:T(128)} %param.22) | copy-start | bytes 196
  20.2 4.5 %copy-start.16 = (f32[16]{0:T(128)S(1)}, f32[16]{0:T(128)}, u32[]{:S(2)}) copy-start(f32[16]{0:T(128)} %copy-done.15) | copy-start | bytes 196
  20.2 4.6 %copy-start.21 = (f32[16]{0:T(128)S(1)}, f32[16]{0:T(128)}, u32[]{:S(2)}) copy-start(f32[16]{0:T(128)} %param.23) | copy-start | bytes 196
  20.2 5.9 %copy-start.18 = (f32[128]{0:T(128)S(1)}, f32[128]{0:T(128)}, u32[]{:S(2)}) copy-start(f32[128]{0:T(128)} %copy-done.17) | copy-start | bytes 1540
  22.3 4.9 %copy-start.5 = (bf16[1,128,1024]{2,1,0:T(8,128)(2,1)S(1)}, bf16[1,128,1024]{2,1,0:T(8,128)(2,1)}, u32[]{:S(2)}) copy-start(bf16[1,128,1024]{2,1,0:T(8,128)(2,1)} %param.16) | copy-start | bytes 786436
  24.1 4.2 %collective-permute-start.2 = (bf16[128,128]{1,0:T(8,128)(2,1)S(1)}, bf16[128,128]{1,0:T(8,128)(2,1)S(1)}, u32[]{:S(2)}, u32[]{:S(2)}) collective-permute-start(bf16[128,128]{1,0:T(8,128)(2,1)S(1)} %get-tuple-element.102), channel_id=1, source_target_pairs={{0,1},{1,0},{2,3},{3,2},{4,5},{5,4},{6,7},{7,6},{8,9},{9,8},{10,11... | collective-permute-start | bytes 98312 | tf_op jit(solution)/shard_map/ppermute | solution.py:20
  27.7 0.8 copy-start.11
  27.8 0.8 copy-start.13
  141.0 9.3 %copy-start.2 = (bf16[1024,1024]{1,0:T(8,128)(2,1)S(1)}, bf16[1024,1024]{1,0:T(8,128)(2,1)}, u32[]{:S(2)}) copy-start(bf16[1024,1024]{1,0:T(8,128)(2,1)} %get-tuple-element.120) | copy-start | bytes 6291460
  150.3 1.3 copy-start.6
  (1 other events, 0.8 us)
